TPU v7x, 256 devices: a whole 4x4x8 slice. The times are simulated.
256 devices in a mesh: row: 8 (over x, z_lo), col: 32 (over z_hi, y, core).
Axes of the slice: x: 4, y: 4, z: 8 (z_hi: 4, z_lo: 2; z = z_hi * 2 + z_lo), core: 2. Of those that a mesh axis runs over, the one named last changes fastest.
Arguments:
- tokens: bfloat16 [512, 12288], P('col', 'row'), may hold values from -6 to 6
- out_grad: bfloat16 [512, 12288], P('col', 'row'), may hold values from -6 to 6
- gate_w: bfloat16 [12288, 28672], P('row', 'col'), may hold values from -0.0546875 to 0.0546875
- up_w: bfloat16 [12288, 28672], P('row', 'col'), may hold values from -0.0546875 to 0.0546875
- down_w: bfloat16 [28672, 12288], P('col', 'row'), may hold values from -0.03125 to 0.03125
- gate_a: float32 [12288, 128], P(('row', 'col')), may hold values from -0.0546875 to 0.0546875
- up_a: float32 [12288, 128], P(('row', 'col')), may hold values from -0.0546875 to 0.0546875
- down_b_t: float32 [12288, 128], P(('row', 'col')), may hold values from -0.25 to 0.25
- gate_b: float32 [128, 28672], P('row', 'col'), may hold values from -0.25 to 0.25
- up_b: float32 [128, 28672], P('row', 'col'), may hold values from -0.25 to 0.25
- down_a_t: float32 [128, 28672], P('row', 'col'), may hold values from -0.03125 to 0.03125
Outputs:
- grad_tokens: float32 [512, 12288], P('col', 'row')
- grad_gate_a: float32 [12288, 128], P(('row', 'col'))
- grad_up_a: float32 [12288, 128], P(('row', 'col'))
- grad_gate_b: float32 [128, 28672], P('row', 'col')
- grad_up_b: float32 [128, 28672], P('row', 'col')
- grad_down_a_t: float32 [128, 28672], P('row', 'col')
- grad_down_b_t: float32 [12288, 128], P(('row', 'col'))
All inputs are finite; a program needn't handle non-finite values.
Results may differ from a plain program's by a relative error of at most 0.0029.
Values may be sent and summed in bfloat16 or wider, within the bound.
No kernel may reach another device: no remote copies, remote signals or barrier semaphores. Data moves between devices by JAX's collectives and lax.ppermute only.
A program may use at most 128 MiB of HBM per device.

v0:
```python
import jax
import jax.numpy as jnp
from jax import lax
from jax.sharding import PartitionSpec as P


def contract_last(left, right, precision_kind):
    return lax.dot_general(
        left,
        right,
        (((1,), (1,)), ((), ())),
        precision=precision_kind,
        preferred_element_type=jnp.float32,
    )


def contract_first(left, right):
    return lax.dot_general(
        left,
        right,
        (((0,), (0,)), ((), ())),
        precision=lax.Precision.HIGHEST,
        preferred_element_type=jnp.float32,
    )


def high_dot(left, right):
    return jnp.dot(left, right, precision=lax.Precision.HIGHEST, preferred_element_type=jnp.float32)


def swiglu_back(sum_gate, sum_up, sum_down, xa_gate, xa_up, dy_rank, b_gate, b_up, a_down):
    gate_pre = sum_gate + high_dot(xa_gate, b_gate)
    up_pre = sum_up + high_dot(xa_up, b_up)
    grad_hidden = sum_down + high_dot(dy_rank, a_down)
    sigma = jax.nn.sigmoid(gate_pre)
    hidden = (gate_pre * sigma * up_pre).astype(jnp.bfloat16)
    d_gate = (grad_hidden * up_pre * sigma * (1.0 + gate_pre * (1.0 - sigma))).astype(jnp.bfloat16)
    d_up = (grad_hidden * gate_pre * sigma).astype(jnp.bfloat16)
    return (hidden, d_gate, d_up)


def body(tokens, out_grad, gate_w, up_w, down_w, gate_a, up_a, down_b_t, gate_b, up_b, down_a_t):
    highest = lax.Precision.HIGHEST
    x_panel, dy_panel = (
        lax.all_gather(tokens, "col", axis=0, tiled=True),
        lax.all_gather(out_grad, "col", axis=0, tiled=True),
    )
    a_gate, a_up, b_down = (
        lax.all_gather(gate_a, "col", axis=0, tiled=True),
        lax.all_gather(up_a, "col", axis=0, tiled=True),
        lax.all_gather(down_b_t, "col", axis=0, tiled=True),
    )
    b_gate, b_up, a_down = (
        lax.all_gather(gate_b, "row", axis=0, tiled=True),
        lax.all_gather(up_b, "row", axis=0, tiled=True),
        lax.all_gather(down_a_t, "row", axis=0, tiled=True),
    )
    xa_gate, xa_up, dy_rank = lax.psum(
        (
            high_dot(x_panel.astype(jnp.float32), a_gate),
            high_dot(x_panel.astype(jnp.float32), a_up),
            high_dot(dy_panel.astype(jnp.float32), b_down),
        ),
        "row",
    )
    part_gate = jnp.dot(x_panel, gate_w, preferred_element_type=jnp.float32)
    part_up = jnp.dot(x_panel, up_w, preferred_element_type=jnp.float32)
    part_down = contract_last(dy_panel, down_w, None)
    sum_gate, sum_up, sum_down = lax.psum((part_gate, part_up, part_down), "row")
    hidden, d_gate, d_up = swiglu_back(
        sum_gate, sum_up, sum_down, xa_gate, xa_up, dy_rank, b_gate, b_up, a_down
    )
    d_gate_float = d_gate.astype(jnp.float32)
    d_up_float = d_up.astype(jnp.float32)
    hidden_float = hidden.astype(jnp.float32)
    g_rank, u_rank, h_rank = lax.psum(
        (
            contract_last(d_gate_float, b_gate, highest),
            contract_last(d_up_float, b_up, highest),
            contract_last(hidden_float, a_down, highest),
        ),
        "col",
    )
    col_rows = x_panel.shape[0] // lax.axis_size("col")
    grad_sum = lax.psum_scatter(
        contract_last(d_gate, gate_w, None) + contract_last(d_up, up_w, None),
        "col",
        scatter_dimension=0,
        tiled=True,
    )
    col_start = lax.axis_index("col") * col_rows
    adapter_term = contract_last(
        lax.dynamic_slice_in_dim(g_rank, col_start, col_rows, 0), a_gate, highest
    )
    adapter_term = adapter_term + contract_last(
        lax.dynamic_slice_in_dim(u_rank, col_start, col_rows, 0), a_up, highest
    )
    grad_tokens = grad_sum + adapter_term
    own_width = gate_a.shape[0]
    feature_start = lax.axis_index("col") * own_width
    x_own = lax.dynamic_slice_in_dim(x_panel, feature_start, own_width, 1).astype(jnp.float32)
    dy_own = lax.dynamic_slice_in_dim(dy_panel, feature_start, own_width, 1).astype(jnp.float32)
    grad_gate_a = contract_first(x_own, g_rank)
    grad_up_a = contract_first(x_own, u_rank)
    grad_down_b_t = contract_first(dy_own, h_rank)
    rank_share = gate_b.shape[0]
    rank_start = lax.axis_index("row") * rank_share
    grad_gate_b = contract_first(
        lax.dynamic_slice_in_dim(xa_gate, rank_start, rank_share, 1), d_gate_float
    )
    grad_up_b = contract_first(
        lax.dynamic_slice_in_dim(xa_up, rank_start, rank_share, 1), d_up_float
    )
    grad_down_a_t = contract_first(
        lax.dynamic_slice_in_dim(dy_rank, rank_start, rank_share, 1), hidden_float
    )
    return (
        grad_tokens,
        grad_gate_a,
        grad_up_a,
        grad_gate_b,
        grad_up_b,
        grad_down_a_t,
        grad_down_b_t,
    )


def solution(mesh):
    placed = (
        P("col", "row"),
        P("col", "row"),
        P("row", "col"),
        P("row", "col"),
        P("col", "row"),
        P(("row", "col"), None),
        P(("row", "col"), None),
        P(("row", "col"), None),
        P("row", "col"),
        P("row", "col"),
        P("row", "col"),
    )
    return jax.shard_map(
        body,
        mesh=mesh,
        in_specs=placed,
        out_specs=(
            P("col", "row"),
            P(("row", "col"), None),
            P(("row", "col"), None),
            P("row", "col"),
            P("row", "col"),
            P("row", "col"),
            P(("row", "col"), None),
        ),
        check_vma=False,
    )
```

profile of v0, /device:TPU:34, one launch (start us, length us, event | category | flops | bytes accessed | tf_op | source)
XLA Modules:
  0.0 864.1 jit_solution(17321661978209097966)
XLA Ops:
  7.2 0.0 copy-start
  7.2 0.0 all-gather.5.cloned.1.call-start
  7.2 0.7 all-gather.5.cloned.1.call-update
  7.9 0.0 all-gather.3.cloned.1.call-start
  8.0 0.7 all-gather.3.cloned.1.call-update
  8.7 0.0 all-reduce.7.cloned.1.call-start
  8.7 54.2 %all_gather.28 = f32[1536,128]{1,0:T(8,128)} all-gather(f32[48,128]{1,0:T(8,128)} %param.17), channel_id=1, replica_groups=mesh['row'=8,'col'=32] {'col'}, dimensions={0}, use_global_device_ids=true | all-gather | bytes 811008 | tf_op jit(solution)/shard_map/all_gather | solution.py:50
  62.9 42.8 %all_gather.30 = f32[1536,128]{1,0:T(8,128)S(1)} all-gather(f32[48,128]{1,0:T(8,128)} %param.16), channel_id=1, replica_groups=mesh['row'=8,'col'=32] {'col'}, dimensions={0}, use_global_device_ids=true | all-gather | bytes 811008 | tf_op jit(solution)/shard_map/all_gather | solution.py:49
  105.7 46.2 %all_gather.25 = f32[1536,128]{1,0:T(8,128)} all-gather(f32[48,128]{1,0:T(8,128)} %param.18), channel_id=1, replica_groups=mesh['row'=8,'col'=32] {'col'}, dimensions={0}, use_global_device_ids=true | all-gather | bytes 811008 | tf_op jit(solution)/shard_map/all_gather | solution.py:51
  151.9 3.9 fusion.27
  155.8 0.0 copy-done.1
  155.8 2.1 fusion.29
  157.9 3.1 fusion.26
  161.0 3.1 fusion.28
  164.1 5.5 fusion.24
  169.6 0.0 copy-done.10
  169.6 2.1 fusion.25
  171.7 0.0 all-reduce.7.cloned.1.call-update
  171.7 0.0 all-reduce.5.cloned.1.call-start
  171.7 32.3 %all_gather.26 = f32[128,896]{1,0:T(8,128)} all-gather(f32[16,896]{1,0:T(8,128)} %param.21), channel_id=1, replica_groups=mesh['row'=8,'col'=32] {'row'}, dimensions={0}, use_global_device_ids=true | all-gather | bytes 516096 | tf_op jit(solution)/shard_map/all_gather | solution.py:56
  204.0 36.0 %all_gather.31 = f32[128,896]{1,0:T(8,128)} all-gather(f32[16,896]{1,0:T(8,128)} %param.19), channel_id=1, replica_groups=mesh['row'=8,'col'=32] {'row'}, dimensions={0}, use_global_device_ids=true | all-gather | bytes 516096 | tf_op jit(solution)/shard_map/all_gather | solution.py:54
  240.0 35.8 %all_gather.29 = f32[128,896]{1,0:T(8,128)} all-gather(f32[16,896]{1,0:T(8,128)} %param.20), channel_id=1, replica_groups=mesh['row'=8,'col'=32] {'row'}, dimensions={0}, use_global_device_ids=true | all-gather | bytes 516096 | tf_op jit(solution)/shard_map/all_gather | solution.py:55
  275.8 180.4 %all-reduce.7.cloned.1.call-done = (f32[512,896]{1,0:T(8,128)}, f32[512,128]{1,0:T(8,128)}, f32[512,896]{1,0:T(8,128)}, f32[512,128]{1,0:T(8,128)}, f32[512,896]{1,0:T(8,128)}, /*index=5*/f32[512,128]{1,0:T(8,128)}) async-done(((f32[512,896]{1,0:T(8,128)}, f32[512,128]{1,0:T(8,128)}, f32[512,896]{1,0:T(8,128)}, f32[512,128]{1,0:T(8,128)}, f32[512,896]{1,0:T(8,128)}, /*index=5*/f32[512,128]{1,0:T(8,128)}), ...) | async-done | bytes 6291472 | tf_op jit(solution)/shard_map/psum | solution.py:69
  456.2 3.5 convolution_add_fusion.4
  459.7 1.6 convolution_add_fusion.2
  461.4 0.1 copy-done.18
  461.4 2.5 multiply_convert_fusion
  464.0 1.6 fusion.31
  465.6 0.0 copy-done.4
  465.6 1.6 fusion.32
  467.2 1.6 fusion.33
  468.8 0.0 all-reduce.5.cloned.1.call-update
  468.9 0.3 reduce-scatter.2.cloned.1.call-start
  469.1 0.0 copy-start.17
  469.1 3.2 fusion.30
  472.3 3.5 convolution_add_fusion
  475.8 0.0 reduce-scatter.2.cloned.1.call-update
  475.8 0.0 copy-start.5
  475.8 2.6 fusion.1
  478.5 2.5 fusion.3
  481.0 1.3 fusion.5
  482.3 273.9 %all-reduce.5.cloned.1.call-done = (f32[512,128]{1,0:T(8,128)}, f32[512,128]{1,0:T(8,128)}, f32[512,128]{1,0:T(8,128)}) async-done(((f32[512,128]{1,0:T(8,128)}, f32[512,128]{1,0:T(8,128)}, f32[512,128]{1,0:T(8,128)}), (f32[512,128]{1,0:T(8,128)}, f32[512,128]{1,0:T(8,128)}, f32[512,128]{1,0:T(8,128)})) %all-reduce.5.cloned.1.call-update) | async-done | bytes 786448 | tf_op jit(solution)/shard_map/psum | solution.py:76
  756.2 2.0 fusion.11
  758.2 2.0 fusion.7
  760.2 2.0 fusion.9
  762.2 2.1 fusion.14
  764.3 90.7 %reduce-scatter.2.cloned.1.call-done = f32[16,1536]{1,0:T(8,128)} async-done(((f32[512,1536]{1,0:T(8,128)}), f32[16,1536]{1,0:T(8,128)}) %reduce-scatter.2.cloned.1.call-update) | async-done | bytes 98320 | tf_op jit(solution)/shard_map/reduce_scatter | solution.py:85
  855.0 2.6 fusion
  (33 shorter events, 0.1 us)
Async XLA Ops:
  7.2 153.8 %copy-start = (bf16[1536,896]{1,0:T(8,128)(2,1)S(1)}, bf16[1536,896]{1,0:T(8,128)(2,1)}, u32[]{:S(2)}) copy-start(bf16[1536,896]{1,0:T(8,128)(2,1)} %param.13) | copy-start | bytes 8257540
  7.2 144.7 %all-gather.5.cloned.1.call-start = ((), (), s32[]{:S(2)}) async-start(), calls=%async_computation.2 | async-start | bytes 1622016 | tf_op jit(solution)/shard_map/all_gather | solution.py:45
  7.9 156.2 %all-gather.3.cloned.1.call-start = ((), (), s32[]{:S(2)}) async-start(), calls=%async_computation.1 | async-start | bytes 1622016 | tf_op jit(solution)/shard_map/all_gather | solution.py:46
  8.7 447.5 %all-reduce.7.cloned.1.call-start = ((), (), s32[]{:S(2)}) async-start(), calls=%async_computation.5 | async-start | bytes 12582912 | tf_op jit(solution)/shard_map/psum | solution.py:69
  151.9 3.9 copy-start.1
  151.9 6.0 copy-start.16
  164.1 5.5 copy-start.9
  164.1 5.5 copy-start.10
  171.7 584.5 %all-reduce.5.cloned.1.call-start = ((), (), s32[]{:S(2)}) async-start(), calls=%async_computation.4 | async-start | bytes 1572864 | tf_op jit(solution)/shard_map/psum | solution.py:76
  456.2 3.5 copy-start.3
  456.2 3.5 copy-start.11
  456.2 3.5 copy-start.13
  459.7 1.7 copy-start.12
  459.7 1.7 copy-start.15
  459.7 1.7 copy-start.18
  463.9 1.7 copy-start.4
  463.9 1.7 copy-start.6
  463.9 3.3 copy-start.8
  464.0 3.3 copy-start.2
  468.9 386.2 %reduce-scatter.2.cloned.1.call-start = ((), (), s32[]{:S(2)}) async-start(), calls=%async_computation.3 | async-start | bytes 3244032 | tf_op jit(solution)/shard_map/reduce_scatter | solution.py:85
  469.1 3.2 copy-start.7
  469.1 3.2 copy-start.17
  475.8 5.2 copy-start.5
  475.8 5.2 copy-start.14
Sparse Core Ops, SparseCore 0:
  10.6 55.2 all-gather.4
  68.4 50.3 all-gather.2
  171.8 284.3 all-reduce.6
  469.0 287.1 all-reduce.4
  760.5 94.5 reduce-scatter.1
where the time goes:
time: 866 us; the launch traced here: 864 us
  waiting for transfers between devices  546 us (63%)
  blocking collectives  247 us (29%)
  matrix products  55.9 us (6%)
  between operations  14 us (2%)
    psum x1, waiting for transfers between devices, body(): lax.psum((contract_last(d_gate_float, b_gate, highest), contract_last(d_u...  274 us
    psum x1, waiting for transfers between devices, body(): lax.psum((part_gate, part_up, part_down), 'row')  180 us
    reduce_scatter x1, waiting for transfers between devices, body(): lax.psum_scatter(contract_last(d_gate, gate_w, None) + contract_last(d_up...  90.7 us
    all_gather x1, blocking collectives, body(): lax.all_gather(up_a, 'col', axis=0, tiled=True)  54.2 us
    all_gather x1, blocking collectives, body(): lax.all_gather(down_b_t, 'col', axis=0, tiled=True)  46.2 us
    all_gather x1, blocking collectives, body(): lax.all_gather(gate_a, 'col', axis=0, tiled=True)  42.8 us
    all_gather x1, blocking collectives, body(): lax.all_gather(gate_b, 'row', axis=0, tiled=True)  36 us
    all_gather x1, blocking collectives, body(): lax.all_gather(up_b, 'row', axis=0, tiled=True)  35.8 us
  transfers between devices with their start and end apart: 5, of which 3 were waited for; matrix products, arithmetic and copies ran while one was open for 4% of the time, Pallas kernels for 0%

commit v1 on v0

v1 whole, which is shorter than its diff:
```python
import jax
import jax.numpy as jnp
from jax import lax
from jax.experimental import pallas as pl
from jax.experimental.pallas import tpu as pltpu
from jax.sharding import Mesh, PartitionSpec as P

ROW = ("x", "zl")
COL = ("zh", "y", "c")
NX, NZL, NZH, NY, NC = 4, 2, 4, 4, 2
NROW = NX * NZL
F32, F16, BF16 = jnp.float32, jnp.float16, jnp.bfloat16
F16_TOP = 32768.0
TINY = 1e-30
SHIFTS = (1, 3, 2)
VMEM = pl.BlockSpec(memory_space=pltpu.VMEM)
SMEM = pl.BlockSpec(memory_space=pltpu.SMEM)
ANY = pl.BlockSpec(memory_space=pl.ANY)
PARAMS = pltpu.CompilerParams(vmem_limit_bytes=48 * 1024 * 1024)


def split(a):
    hi = a.astype(BF16)
    return hi, (a - hi.astype(F32)).astype(BF16)


def dot(a, b, dims=((1,), (0,))):
    return lax.dot_general(a, b, (dims, ((), ())), preferred_element_type=F32)


def dot2(a, b, dims=((1,), (0,))):
    bh, bl = split(b)
    return dot(a, bh, dims) + dot(a, bl, dims)


def dot3(a, b, dims=((1,), (0,))):
    ah, al = split(a)
    bh, bl = split(b)
    return dot(ah, bh, dims) + (dot(ah, bl, dims) + dot(al, bh, dims))


def shape(dims, kind):
    return jax.ShapeDtypeStruct(dims, kind)


def from_next(a, axis, n, s):
    return lax.ppermute(a, axis, [(j, (j - s) % n) for j in range(n)])


def to_next(a, axis, n, s):
    return lax.ppermute(a, axis, [(j, (j + s) % n) for j in range(n)])


def exchange(wide, axis):
    return lax.all_to_all(wide, axis, split_axis=0, concat_axis=0)


def cost(flops, *arrays):
    moved = sum(a.size * a.dtype.itemsize for a in arrays)
    return pl.CostEstimate(flops=flops, bytes_accessed=moved, transcendentals=0)


def pack(tokens, out_grad, *factors):
    own, width = out_grad.shape
    own_features, rank = factors[0].shape
    ranks = rank * len(factors)
    groups = own_features // own

    def kernel(x, dy, *refs):
        out = refs[-1]
        out[:, :width] = x[...]
        out[:, width : 2 * width] = dy[...]
        halves = [split(ref[...]) for ref in refs[:-1]]
        order = [h[0] for h in halves[:-1]] + [h[1] for h in halves[:-1]] + list(halves[-1])
        for k in range(groups):
            for i, value in enumerate(order):
                at = 2 * width + k * 2 * ranks + i * rank
                out[:, at : at + rank] = value[k * own : (k + 1) * own]

    return pl.pallas_call(
        kernel,
        out_shape=shape((own, 2 * width + groups * 2 * ranks), BF16),
        in_specs=[VMEM] * (2 + len(factors)),
        out_specs=VMEM,
    )(tokens, out_grad, *factors)


def join_rows(here, cut, *parts):
    rows, lanes = parts[0].shape

    def kernel(here, *refs):
        left, right = refs[-2:]
        for s, ref in enumerate(refs[:-2]):
            at = pl.multiple_of(lax.rem(here[0] + s, len(parts)) * rows, rows)
            left[pl.ds(at, rows), :] = ref[:, :cut]
            right[pl.ds(at, rows), :] = ref[:, cut:]

    return pl.pallas_call(
        kernel,
        out_shape=(
            shape((rows * len(parts), cut), parts[0].dtype),
            shape((rows * len(parts), lanes - cut), parts[0].dtype),
        ),
        in_specs=[SMEM] + [VMEM] * len(parts),
        out_specs=(VMEM, VMEM),
    )(here, *parts)


def panel_moves(place, pieces, first, size, target, sems):
    y, c = place[1], place[2]
    moves = []
    for dc in range(NC):
        for d in range(NY):
            block = lax.rem(c + dc, NC) * NY + lax.rem(y + d, NY)
            piece = pieces[dc * NY + d]
            rows = piece.shape[0]
            moves.append(
                pltpu.make_async_copy(
                    piece.at[:, pl.ds(first, size)],
                    target.at[pl.ds(pl.multiple_of(block * rows, rows), rows)],
                    sems.at[dc * NY + d],
                )
            )
    return moves


def scaled(part, at, size, values, index, exponents):
    rows = part.shape[0]
    step = rows // 4
    top = jnp.float32(TINY)
    for k in range(0, rows, step):
        value = values(slice(k, k + step))
        part[k : k + step, at : at + size] = value
        top = jnp.maximum(top, jnp.max(jnp.abs(value)))
    exponent = jnp.ceil(jnp.log2(jnp.full((1, 128), top, F32))) - 15.0
    scale = jnp.exp2(-exponent)[:, :1]
    for k in range(0, rows, step):
        part[k : k + step, at : at + size] = part[k : k + step, at : at + size] * scale
    lane = lax.broadcasted_iota(jnp.int32, (1, 128), 1)
    return jnp.where(lane // 16 == index, exponent, exponents)


def forward_x(place, pieces, gate_w, up_w):
    quarter = pieces[0].shape[0]
    width, units = gate_w.shape
    rows = quarter * NY * NC

    def kernel(place, *refs):
        piece = refs[:8]
        gate, up, part_out, x_out, exponents_out = refs[8:13]
        part, x, w_gate, w_up, sem_x, sem_w, sem_o = refs[13:]
        moves = panel_moves(place, piece, 0, width, x, sem_x)
        load = [
            pltpu.make_async_copy(a, b, sem_w.at[i])
            for i, (a, b) in enumerate(((gate, w_gate), (up, w_up)))
        ]
        store = [
            pltpu.make_async_copy(
                part.at[:, pl.ds(i * units, units)],
                part_out.at[:, pl.ds(i * units, units)],
                sem_o.at[i],
            )
            for i in range(2)
        ]
        store_x = pltpu.make_async_copy(x, x_out, sem_o.at[2])
        for copy in moves + load:
            copy.start()
        for copy in moves + load[:1]:
            copy.wait()
        store_x.start()
        exponents = jnp.zeros((1, 128), F32)
        exponents = scaled(part, 0, units, lambda at: dot(x[at, :], w_gate[...]), 0, exponents)
        store[0].start()
        load[1].wait()
        exponents = scaled(part, units, units, lambda at: dot(x[at, :], w_up[...]), 1, exponents)
        store[1].start()
        exponents_out[...] = jnp.broadcast_to(exponents, (8, 128))
        for copy in store + [store_x]:
            copy.wait()

    return pl.pallas_call(
        kernel,
        out_shape=(
            shape((rows, 2 * units), F32),
            shape((rows, width), BF16),
            shape((8, 128), F32),
        ),
        in_specs=[SMEM] + [ANY] * 10,
        out_specs=(ANY, ANY, VMEM),
        scratch_shapes=[
            pltpu.VMEM((rows, 2 * units), F32),
            pltpu.VMEM((rows, width), BF16),
            pltpu.VMEM(gate_w.shape, BF16),
            pltpu.VMEM(up_w.shape, BF16),
            pltpu.SemaphoreType.DMA((8,)),
            pltpu.SemaphoreType.DMA((2,)),
            pltpu.SemaphoreType.DMA((3,)),
        ],
        compiler_params=PARAMS,
        cost_estimate=cost(12 * rows * width * units, gate_w, up_w),
    )(place, *pieces, gate_w, up_w)


def forward_dy(place, pieces, x, down_w, exponents, ranks, own_features):
    quarter, lanes = pieces[0].shape
    own = quarter // NZH
    rows, width = x.shape
    units = down_w.shape[0]
    rank = ranks // 3
    groups = own_features // own

    def kernel(place, *refs):
        piece = refs[:8]
        x_in, down, exponents_in, part, dy_out, factors = refs[8:14]
        x, dy, packed, w_down, sem_dy, sem_a, sem_w, sem_o = refs[14:]
        move_dy = panel_moves(place, piece, 0, width, dy, sem_dy)
        move_a = panel_moves(place, piece, width, lanes - width, packed, sem_a)
        load = [
            pltpu.make_async_copy(down, w_down, sem_w.at[0]),
            pltpu.make_async_copy(x_in, x, sem_w.at[1]),
        ]
        store_dy = pltpu.make_async_copy(dy, dy_out, sem_o)
        for copy in move_dy + load[:1] + move_a + load[1:]:
            copy.start()
        for copy in move_dy + load[:1]:
            copy.wait()
        store_dy.start()
        exponents = exponents_in[0:1, :]
        exponents = scaled(
            part, 0, units, lambda at: dot(dy[at, :], w_down[...], ((1,), (1,))), 2, exponents
        )
        for copy in move_a + load[1:]:
            copy.wait()
        for c in range(NC):
            for y in range(NY):
                for zh in range(NZH):
                    to = ((zh * NY + y) * NC + c) * own_features
                    at = ((c * NY + y) * NZH + zh) * own
                    for k in range(groups):
                        factors[to + k * own : to + (k + 1) * own, :] = packed[
                            at : at + own, k * 2 * ranks : (k + 1) * 2 * ranks
                        ]
        xa = dot(x[...], factors[:, : 2 * rank]) + dot(x[...], factors[:, 2 * rank : 4 * rank])
        dya = dot(dy[...], factors[:, 4 * rank :])
        dya = dya[:, :rank] + dya[:, rank:]
        values = (xa[:, :rank], xa[:, rank:], dya)
        for i, value in enumerate(values):
            exponents = scaled(
                part, units + i * rank, rank, lambda at: value[at, :], 3 + i, exponents
            )
        part[:, units + ranks :] = jnp.broadcast_to(exponents, (rows, 128))
        store_dy.wait()

    return pl.pallas_call(
        kernel,
        out_shape=(
            shape((rows, units + ranks + 128), F32),
            shape((rows, width), BF16),
            shape((width, 2 * ranks), BF16),
        ),
        in_specs=[SMEM] + [ANY] * 10 + [VMEM],
        out_specs=(VMEM, ANY, VMEM),
        scratch_shapes=[
            pltpu.VMEM((rows, width), BF16),
            pltpu.VMEM((rows, width), BF16),
            pltpu.VMEM((rows, lanes - width), BF16),
            pltpu.VMEM(down_w.shape, BF16),
            pltpu.SemaphoreType.DMA((8,)),
            pltpu.SemaphoreType.DMA((8,)),
            pltpu.SemaphoreType.DMA((2,)),
            pltpu.SemaphoreType.DMA,
        ],
        compiler_params=PARAMS,
        cost_estimate=cost(12 * rows * width * units, down_w, x),
    )(place, *pieces, x, down_w, exponents)


def swiglu_back(first, second, b_parts):
    per, lanes = second.shape[1:]
    share, units = b_parts.shape[1] // 3, b_parts.shape[2]
    rank = share * NROW
    ranks = 3 * rank
    sizes = [units] * 3 + [rank] * 3
    starts = [0, units, 0, units, units + rank, units + 2 * rank]

    def kernel(first, second, b_parts, wide, g_out, factor_out, b):
        for i in range(3):
            for r in range(NROW):
                b[i, r * share : (r + 1) * share, :] = b_parts[r, i * share : (i + 1) * share, :]
        scales = [jnp.exp2(second[r, 0:1, lanes - 128 :]) for r in range(NROW)]

        def total(i):
            value = 0.0
            sums = first if i < 2 else second
            for r in range(NROW):
                part = sums[r, :, starts[i] : starts[i] + sizes[i]]
                value = value + part * scales[r][:, 16 * i : 16 * i + 1]
            return value

        products = [total(3 + i) for i in range(3)]
        gate_pre, up_pre, grad_hidden = (total(i) + dot3(products[i], b[i]) for i in range(3))
        sigma = 1.0 / (1.0 + jnp.exp(-gate_pre))
        hidden = (gate_pre * sigma * up_pre).astype(BF16)
        d_gate = (grad_hidden * up_pre * sigma * (1.0 + gate_pre * (1.0 - sigma))).astype(BF16)
        d_up = (grad_hidden * gate_pre * sigma).astype(BF16)
        for r in range(NROW):
            wide[r, :, :units] = d_gate
            wide[r, :, units:] = d_up
        for i, d in enumerate((d_gate, d_up, hidden)):
            g_out[:, i * rank : (i + 1) * rank] = dot2(d, b[i], ((1,), (1,)))
            hi, lo = split(products[i].T)
            grad = dot(hi, d) + dot(lo, d)
            for r in range(NROW):
                factor_out[r, i * share : (i + 1) * share, :] = grad[
                    r * share : (r + 1) * share
                ].astype(BF16)

    return pl.pallas_call(
        kernel,
        out_shape=(
            shape((NROW, per, 2 * units), BF16),
            shape((per, ranks), F32),
            shape(b_parts.shape, BF16),
        ),
        in_specs=[VMEM] * 3,
        out_specs=(VMEM,) * 3,
        scratch_shapes=[pltpu.VMEM((3, rank, units), F32)],
        compiler_params=PARAMS,
        cost_estimate=cost(24 * per * rank * units, first, second),
    )(first, second, b_parts)


def backward(which, d_all, gate_w, up_w):
    half = d_all.shape[0] // NC
    width, units = gate_w.shape

    def kernel(which, d, gate, up, out):
        at = pl.ds(pl.multiple_of(which[0] * half, half), half)
        out[...] = dot(d[at, :units], gate[...], ((1,), (1,))) + dot(
            d[at, units:], up[...], ((1,), (1,))
        )

    return pl.pallas_call(
        kernel,
        out_shape=shape((half, width), F32),
        in_specs=[SMEM] + [VMEM] * 3,
        out_specs=VMEM,
        compiler_params=PARAMS,
        cost_estimate=cost(4 * half * width * units, gate_w, up_w),
    )(which, d_all, gate_w, up_w)


def add_and_cut(here, kind, *parts):
    rows, width = parts[0].shape
    block = rows // 4

    def kernel(here, *refs):
        ins, outs = refs[: len(parts)], refs[len(parts) :]
        for s, out in zip((0,) + SHIFTS, outs):
            at = pl.ds(pl.multiple_of(lax.rem(here[0] + s, 4) * block, block), block)
            total = ins[0][at, :].astype(F32)
            for ref in ins[1:]:
                total = total + ref[at, :].astype(F32)
            out[...] = total.astype(out.dtype)

    return pl.pallas_call(
        kernel,
        out_shape=(shape((block, width), F32),) + (shape((block, width), kind),) * 3,
        in_specs=[SMEM] + [VMEM] * len(parts),
        out_specs=(VMEM,) * 4,
        compiler_params=PARAMS,
    )(here, *parts)


def merge(factor_parts, g):
    share, units = factor_parts.shape[1:]
    per, ranks = g.shape

    def kernel(parts, g, out):
        hi, lo = split(g[...])
        for r in range(NROW):
            out[r, :share, :] = parts[r]
            out[r, share:, :ranks] = hi
            out[r, share:, ranks : 2 * ranks] = lo
            out[r, share:, 2 * ranks :] = jnp.zeros((per, units - 2 * ranks), BF16)

    return pl.pallas_call(
        kernel,
        out_shape=shape((NROW, share + per, units), BF16),
        in_specs=[VMEM] * 2,
        out_specs=VMEM,
    )(factor_parts, g)


def select(place, x, dy, own_features):
    rows, width = x.shape

    def kernel(place, x, dy, out):
        y, c = place[1], place[2]
        row = lax.broadcasted_iota(jnp.int32, (own_features, width), 0)
        lane = lax.broadcasted_iota(jnp.int32, (own_features, width), 1)
        for zh in range(NZH):
            start = ((zh * NY + y) * NC + c) * own_features
            pick = jnp.where(lane == row + start, 1.0, 0.0).astype(BF16)
            for i, panel in enumerate((x, dy)):
                at = (i * NZH + zh) * own_features
                out[at : at + own_features, :] = dot(pick, panel[...], ((1,), (1,))).astype(BF16)

    return pl.pallas_call(
        kernel,
        out_shape=shape((2 * NZH * own_features, rows), BF16),
        in_specs=[SMEM, VMEM, VMEM],
        out_specs=VMEM,
        compiler_params=PARAMS,
        cost_estimate=cost(4 * NZH * own_features * rows * width, x, dy),
    )(place, x, dy)


def rank_grads(place, selected, merged, factors, ranks):
    features = selected.shape[0] // 2
    rows = selected.shape[1]
    per = rows // NROW
    rank = ranks // 3
    share = merged.shape[1] - per
    width = factors.shape[0]

    def kernel(place, selected, merged, factors, grads, adapter, g):
        for r in range(NROW):
            g[r * per : (r + 1) * per, :] = merged[r, share:, : 2 * ranks]
        hi, lo = g[:, :ranks], g[:, ranks:]
        xs, dys = selected[:features, :], selected[features:, :]
        grads[:, : 2 * rank] = dot(xs, hi[:, : 2 * rank]) + dot(xs, lo[:, : 2 * rank])
        grads[:, 2 * rank :] = dot(dys, hi[:, 2 * rank :]) + dot(dys, lo[:, 2 * rank :])
        block = place[2] * NY + place[1]
        own = g[pl.ds(pl.multiple_of(block * per, per), per), :]
        gh, gl = own[:, : 2 * rank], own[:, ranks : ranks + 2 * rank]
        ah, al = factors[:, : 2 * rank], factors[:, 2 * rank : 4 * rank]
        last = ((1,), (1,))
        adapter[...] = dot(gh, ah, last) + (dot(gl, ah, last) + dot(gh, al, last))

    return pl.pallas_call(
        kernel,
        out_shape=(shape((features, ranks), F32), shape((per, width), F32)),
        in_specs=[SMEM] + [VMEM] * 3,
        out_specs=(VMEM, VMEM),
        scratch_shapes=[pltpu.VMEM((rows, 2 * ranks), BF16)],
        compiler_params=PARAMS,
    )(place, selected, merged, factors)


def cut_last(here, grads, *parts):
    rows, width = parts[0].shape
    block = rows // NZH
    features = grads.shape[0] // NZH
    ranks = grads.shape[1]
    groups = features // block

    def kernel(here, grads, *refs):
        ins, outs = refs[: len(parts)], refs[len(parts) :]
        for s, out in zip((0,) + SHIFTS, outs):
            to = lax.rem(here[0] + s, NZH)
            at = pl.ds(pl.multiple_of(to * block, block), block)
            total = ins[0][at, :].astype(F32)
            for ref in ins[1:]:
                total = total + ref[at, :].astype(F32)
            out[:, :width] = total
            for k in range(groups):
                at = pl.ds(pl.multiple_of(to * features + k * block, block), block)
                out[:, width + k * ranks : width + (k + 1) * ranks] = grads[at, :]

    return pl.pallas_call(
        kernel,
        out_shape=(shape((block, width + groups * ranks), F32),) * 4,
        in_specs=[SMEM] + [VMEM] * (1 + len(parts)),
        out_specs=(VMEM,) * 4,
        compiler_params=PARAMS,
    )(here, grads, *parts)


def finish(width, rank, *parts):
    own, lanes = parts[0].shape
    ranks = 3 * rank
    groups = (lanes - width) // ranks

    def kernel(*refs):
        ins, (tokens, *factors) = refs[:4], refs[4:]
        total = (ins[0][...] + ins[1][...]) + (ins[2][...] + ins[3][...])
        tokens[...] = total[:, :width]
        for k in range(groups):
            for i, out in enumerate(factors):
                at = width + k * ranks + i * rank
                out[k * own : (k + 1) * own, :] = total[:, at : at + rank]

    return pl.pallas_call(
        kernel,
        out_shape=(shape((own, width), F32),) + (shape((own * groups, rank), F32),) * 3,
        in_specs=[VMEM] * 4,
        out_specs=(VMEM,) * 4,
    )(*parts)


def after(value, *others):
    return lax.optimization_barrier((value,) + others)[0]


def body(tokens, out_grad, gate_w, up_w, down_w, gate_a, up_a, down_b_t, gate_b, up_b, down_a_t):
    own, width = tokens.shape
    units = gate_w.shape[1]
    own_features, rank = gate_a.shape
    zh, y, c = (lax.axis_index(a) for a in COL)
    row = lax.axis_index(ROW)
    place = jnp.stack([zh, y, c, row]).astype(jnp.int32)

    at_zh, at_y, at_c, at_other = (
        v.reshape(1).astype(jnp.int32) for v in (zh, y, c, (c + 1) % NC)
    )
    ranks = 3 * rank

    mine = pack(tokens, out_grad, gate_a, up_a, down_b_t)
    got = {0: mine}
    for s in SHIFTS:
        got[s] = from_next(mine, "zh", NZH, s)
    near, late = join_rows(at_zh, width, *[got[s] for s in range(NZH)])

    def from_y(a):
        got = {0: a}
        for s in SHIFTS:
            got[s] = from_next(a, "y", NY, s)
        return [got[s] for s in range(NY)]

    def with_core(pieces):
        return pieces + [from_next(p, "c", NC, 1) for p in pieces]

    b_own = after(jnp.concatenate([gate_b, up_b, down_a_t], axis=0), near)
    b_parts = exchange(jnp.broadcast_to(b_own[None], (NROW,) + b_own.shape), ROW)
    pieces = from_y(near)
    late_pieces = from_y(after(late, pieces[2]))
    pieces = with_core(pieces)

    def sums(part):
        sent = part.astype(F16).reshape(NROW, rows // NROW, part.shape[1])
        return exchange(sent, ROW).astype(F32)

    part_x, x, exponents = forward_x(place, pieces, gate_w, up_w)
    rows = x.shape[0]
    part_x, b_parts, *late_pieces = lax.optimization_barrier((part_x, b_parts, *late_pieces))
    part_dy, dy, factors = forward_dy(
        place, with_core(late_pieces), x, down_w, exponents, ranks, own_features
    )
    sums_x = sums(part_x)
    sums_x, part_dy = lax.optimization_barrier((sums_x, part_dy))
    selected = select(place, x, dy, own_features)
    wide, g, factor_parts = swiglu_back(sums_x, sums(part_dy), b_parts)

    d_all = exchange(wide, ROW).reshape(rows, 2 * units)

    g = g + from_next(g, "c", NC, 1)
    g = g + sum(from_next(g, "y", NY, s) for s in SHIFTS)
    merged = merge(factor_parts, g)
    d_all, merged, selected = lax.optimization_barrier((d_all, merged, selected))
    merged = exchange(merged, ROW)

    sent = backward(at_other, d_all, gate_w, up_w)
    other = from_next(sent, "c", NC, 1)
    kept = backward(at_c, after(d_all, sent), gate_w, up_w)
    kept, *sends = add_and_cut(at_y, BF16, kept, other)
    others = [to_next(a, "y", NY, s) for s, a in zip(SHIFTS, sends)]

    grads, adapter = rank_grads(place, selected, merged, factors, ranks)
    kept, *sends = cut_last(at_zh, grads, kept, *others, adapter)
    others = [to_next(a, "zh", NZH, s) for s, a in zip(SHIFTS, sends)]
    grad_tokens, grad_gate_a, grad_up_a, grad_down_b_t = finish(width, rank, kept, *others)

    share = gate_b.shape[0]
    factor_grads = merged[:, : 3 * share].astype(F32).sum(0)
    grad_b = [factor_grads[i * share : (i + 1) * share] for i in range(3)]
    return (grad_tokens, grad_gate_a, grad_up_a, *grad_b, grad_down_b_t)


def solution(mesh):
    fine = Mesh(mesh.devices.reshape(NX, NZL, NZH, NY, NC), ROW + COL)
    tiled = P(COL, ROW)
    weight = P(ROW, COL)
    factor = P(ROW + COL, None)
    return jax.shard_map(
        body,
        mesh=fine,
        in_specs=(tiled, tiled, weight, weight, tiled, factor, factor, factor, weight, weight, weight),
        out_specs=(tiled, factor, factor, weight, weight, weight, factor),
        check_vma=False,
    )
```

time: 866 us -> 225 us (0.26)
  waiting for transfers between devices: 546 us -> 70.1 us
  blocking collectives: 247 us -> 22.6 us
  starting transfers between devices: 0.42 us -> 59.1 us
  matrix products: 55.9 us -> 0 us
  Pallas kernels: 0 us -> 45.3 us
  local copies, waits for them, and re-layouts: 0.14 us -> 14.8 us
  between operations: 14 us -> 0.85 us
  other arithmetic: 0 us -> 10.9 us
    psum x2 -> x0, waiting for transfers between devices: 454 us -> none  [the longest x1 274 us: body(): lax.psum((contract_last(d_gate_float, b_gate, highest), contract_last(d_u...]
    all_gather x6 -> x0, blocking collectives: 247 us -> none  [the longest x1 54.2 us: body(): lax.all_gather(up_a, 'col', axis=0, tiled=True)]
    reduce_scatter x1 -> x0, waiting for transfers between devices: 90.7 us -> none  [body(): lax.psum_scatter(contract_last(d_gate, gate_w, None) + contract_last(d_up...]
    dot_general x22 -> x0, matrix products: 55.9 us -> none  [the longest x8 21.6 us: contract_last(): lax.dot_general(left, right, (((1,), (1,)), ((), ())), precision=precisio...]
    ppermute x0 -> x28, waiting for transfers between devices: none -> 50.2 us  [the longest x22 37.2 us: from_next(): return lax.ppermute(a, axis, [(j, (j - s) % n) for j in range(n)])]
    pallas_call x0 -> x13, Pallas kernels: none -> 45.3 us  [the longest x1 10.6 us: forward_dy(): pl.pallas_call(kernel, out_shape=(shape((rows, units + ranks + 128), F32)...]
    ppermute x0 -> x28, starting transfers between devices: none -> 35.8 us  [the longest x22 22.4 us: from_next(): return lax.ppermute(a, axis, [(j, (j - s) % n) for j in range(n)])]
    all_to_all x0 -> x4, starting transfers between devices: none -> 23.3 us  [exchange(): return lax.all_to_all(wide, axis, split_axis=0, concat_axis=0)]
  transfers between devices with their start and end apart: 5 -> 32, of which waited for: 3 -> 18; matrix products, arithmetic and copies ran while one was open for 4% -> 1% of each run, Pallas kernels for 0% -> 16%
where the time goes in v1:
time: 225 us; the launch traced here: 224 us
  waiting for transfers between devices  70.1 us (31%)
  starting transfers between devices  59.1 us (26%)
  Pallas kernels  45.3 us (20%)
  blocking collectives  22.6 us (10%)
  local copies, waits for them, and re-layouts  14.8 us (7%)
  other arithmetic  10.9 us (5%)
    ppermute x22, waiting for transfers between devices, from_next(): return lax.ppermute(a, axis, [(j, (j - s) % n) for j in range(n)])  37.2 us
    all_to_all x4, starting transfers between devices, exchange(): return lax.all_to_all(wide, axis, split_axis=0, concat_axis=0)  23.3 us
    all_to_all x1, blocking collectives, exchange(): return lax.all_to_all(wide, axis, split_axis=0, concat_axis=0)  22.6 us
    ppermute x22, starting transfers between devices, from_next(): return lax.ppermute(a, axis, [(j, (j - s) % n) for j in range(n)])  22.4 us
    all_to_all x4, waiting for transfers between devices, exchange(): return lax.all_to_all(wide, axis, split_axis=0, concat_axis=0)  19.9 us
    ppermute x6, starting transfers between devices, to_next(): return lax.ppermute(a, axis, [(j, (j + s) % n) for j in range(n)])  13.4 us
    ppermute x6, waiting for transfers between devices, to_next(): return lax.ppermute(a, axis, [(j, (j + s) % n) for j in range(n)])  13 us
    unnamed x50, local copies, waits for them, and re-layouts  13 us
  transfers between devices with their start and end apart: 32, of which 18 were waited for; matrix products, arithmetic and copies ran while one was open for 1% of the time, Pallas kernels for 16%

profile of v1, /device:TPU:34, one launch (start us, length us, event | category | flops | bytes accessed | tf_op | source)
XLA Modules:
  0.0 223.7 jit_solution(5406247031435701730)
XLA Ops:
  0.6 1.5 shard_map.162.refs_0_
  2.2 5.4 %collective-permute-start = (bf16[16,5376]{1,0:T(8,128)(2,1)}, bf16[16,5376]{1,0:T(8,128)(2,1)S(1)}, u32[]{:S(2)}, u32[]{:S(2)}) collective-permute-start(bf16[16,5376]{1,0:T(8,128)(2,1)} %shard_map.162.refs_0_), channel_id=1, source_target_pairs={{0,24},{8,0},{16,8},{24,16},{1,25},{9,1},{17,9},{25,17},{2,26},{10... | collective-permute-start | bytes 516104 | tf_op jit(solution)/shard_map/ppermute | solution.py:47
  7.6 1.4 collective-permute-start.1
  9.0 2.4 %collective-permute-start.2 = (bf16[16,5376]{1,0:T(8,128)(2,1)}, bf16[16,5376]{1,0:T(8,128)(2,1)S(1)}, u32[]{:S(2)}, u32[]{:S(2)}) collective-permute-start(bf16[16,5376]{1,0:T(8,128)(2,1)} %shard_map.162.refs_0_), channel_id=1, source_target_pairs={{0,8},{8,16},{16,24},{24,0},{1,9},{9,17},{17,25},{25,1},{2,10},{10... | collective-permute-start | bytes 516104 | tf_op jit(solution)/shard_map/ppermute | solution.py:47
  12.3 4.4 %collective-permute-done.refs_1_ = bf16[16,5376]{1,0:T(8,128)(2,1)S(1)} collective-permute-done((bf16[16,5376]{1,0:T(8,128)(2,1)}, bf16[16,5376]{1,0:T(8,128)(2,1)S(1)}, u32[]{:S(2)}, u32[]{:S(2)}) %collective-permute-start) | collective-permute-done | bytes 172064 | tf_op jit(solution)/shard_map/ppermute | solution.py:47
  16.6 7.8 %collective-permute-done.1.refs_2_ = bf16[16,5376]{1,0:T(8,128)(2,1)S(1)} collective-permute-done((bf16[16,5376]{1,0:T(8,128)(2,1)}, bf16[16,5376]{1,0:T(8,128)(2,1)S(1)}, u32[]{:S(2)}, u32[]{:S(2)}) %collective-permute-start.1) | collective-permute-done | bytes 172064 | tf_op jit(solution)/shard_map/ppermute | solution.py:47
  25.6 2.1 shard_map.163
  27.7 1.2 broadcast_in_dim.2
  28.9 6.0 %all-to-all-start = ((f32[8,48,896]{2,1,0:T(8,128)}), f32[8,48,896]{2,1,0:T(8,128)}, u32[]{:S(2)}, u32[]{:S(2)}) async-start(f32[8,48,896]{2,1,0:T(8,128)} %broadcast_in_dim.2), calls=%async_computation | async-start | bytes 2752512 | tf_op jit(solution)/shard_map/all_to_all | solution.py:55
  34.9 3.2 %collective-permute-start.4 = (bf16[64,1536]{1,0:T(8,128)(2,1)S(1)}, bf16[64,1536]{1,0:T(8,128)(2,1)}, u32[]{:S(2)}, u32[]{:S(2)}) collective-permute-start(bf16[64,1536]{1,0:T(8,128)(2,1)S(1)} %copy-done.17), channel_id=1, source_target_pairs={{0,4},{2,6},{4,0},{6,2},{1,5},{3,7},{5,1},{7,3},{8,12},{10,14},{12... | collective-permute-start | bytes 589832 | tf_op jit(solution)/shard_map/ppermute | solution.py:47
  40.1 4.2 %collective-permute-done.4.refs_2_ = bf16[64,1536]{1,0:T(8,128)(2,1)} collective-permute-done((bf16[64,1536]{1,0:T(8,128)(2,1)S(1)}, bf16[64,1536]{1,0:T(8,128)(2,1)}, u32[]{:S(2)}, u32[]{:S(2)}) %collective-permute-start.4) | collective-permute-done | bytes 196640 | tf_op jit(solution)/shard_map/ppermute | solution.py:47
  44.3 2.5 %collective-permute-done.3.refs_1_ = bf16[64,1536]{1,0:T(8,128)(2,1)} collective-permute-done((bf16[64,1536]{1,0:T(8,128)(2,1)S(1)}, bf16[64,1536]{1,0:T(8,128)(2,1)}, u32[]{:S(2)}, u32[]{:S(2)}) %collective-permute-start.3) | collective-permute-done | bytes 196640 | tf_op jit(solution)/shard_map/ppermute | solution.py:47
  47.5 2.7 %collective-permute-start.10 = (bf16[64,3840]{1,0:T(8,128)(2,1)S(1)}, bf16[64,3840]{1,0:T(8,128)(2,1)S(1)}, u32[]{:S(2)}, u32[]{:S(2)}) collective-permute-start(bf16[64,3840]{1,0:T(8,128)(2,1)S(1)} %copy-done.12), channel_id=1, source_target_pairs={{0,6},{2,0},{4,2},{6,4},{1,7},{3,1},{5,3},{7,5},{8,14},{10,8},{12,... | collective-permute-start | bytes 1474568 | tf_op jit(solution)/shard_map/ppermute | solution.py:47
  51.3 7.8 %shard_map.164 = (f32[512,1792]{1,0:T(8,128)}, bf16[512,1536]{1,0:T(8,128)(2,1)S(1)}, f32[8,128]{1,0:T(8,128)S(1)}) custom-call(s32[4]{0:T(128)S(1)} %pad_add_fusion.place, bf16[64,1536]{1,0:T(8,128)(2,1)S(1)} %copy-done.17, bf16[64,1536]{1,0:T(8,128)(2,1)} %collective-permute-done.3.refs_1_, bf16[64,1536]{1,0:T(8,128)(2,1)} %collective-permute-done.4.refs_2_, ...), custom_call_target="tpu_custom_call" | custom-call | flops 8455716864 | bytes 5505024 | tf_op jit(solution)/shard_map/pallas_call | solution.py:181
  60.3 11.1 %collective-permute-done.10.refs_1_ = bf16[64,3840]{1,0:T(8,128)(2,1)S(1)} collective-permute-done((bf16[64,3840]{1,0:T(8,128)(2,1)S(1)}, bf16[64,3840]{1,0:T(8,128)(2,1)S(1)}, u32[]{:S(2)}, u32[]{:S(2)}) %collective-permute-start.10) | collective-permute-done | bytes 491552 | tf_op jit(solution)/shard_map/ppermute | solution.py:47
  73.0 2.2 collective-permute-done.12.refs_3_
  75.2 3.6 %convert_element_type.15 = f16[512,1792]{1,0:T(8,128)(2,1)} convert(f32[512,1792]{1,0:T(8,128)} %get-tuple-element.51) | non-fusion elementwise | flops 917504 | bytes 5505024 | tf_op jit(solution)/shard_map/convert_element_type | solution.py:541
  78.7 5.8 %all-to-all-start.1 = ((f16[8,64,1792]{2,1,0:T(8,128)(2,1)}), f16[8,64,1792]{2,1,0:T(8,128)(2,1)}, u32[]{:S(2)}, u32[]{:S(2)}) async-start(f16[8,64,1792]{2,1,0:T(8,128)(2,1)} %bitcast.4), calls=%async_computation.1 | async-start | bytes 3670016 | tf_op jit(solution)/shard_map/all_to_all | solution.py:55
  86.4 1.4 collective-permute-done.14.refs_5_
  88.5 10.6 %shard_map.165 = (f32[512,1408]{1,0:T(8,128)}, bf16[512,1536]{1,0:T(8,128)(2,1)S(1)}, bf16[1536,768]{1,0:T(8,128)(2,1)}) custom-call(s32[4]{0:T(128)S(1)} %pad_add_fusion.place, bf16[64,3840]{1,0:T(8,128)(2,1)S(1)} %copy-done.12, bf16[64,3840]{1,0:T(8,128)(2,1)S(1)} %copy-done.14, bf16[64,3840]{1,0:T(8,128)(2,1)S(1)} %copy-done.16, ...), custom_call_target="tpu_custom_call" | custom-call | flops 8455716864 | bytes 4325376 | tf_op jit(solution)/shard_map/pallas_call | solution.py:254
  99.2 1.1 copy-done.6
  100.3 6.6 %all-to-all-done.1 = f16[8,64,1792]{2,1,0:T(8,128)(2,1)} async-done(((f16[8,64,1792]{2,1,0:T(8,128)(2,1)}), f16[8,64,1792]{2,1,0:T(8,128)(2,1)}, u32[]{:S(2)}, u32[]{:S(2)}) %all-to-all-start.1) | async-done | bytes 1835040 | tf_op jit(solution)/shard_map/all_to_all | solution.py:55
  106.9 3.6 %convert_element_type.16.first = f32[8,64,1792]{2,1,0:T(8,128)} convert(f16[8,64,1792]{2,1,0:T(8,128)(2,1)} %all-to-all-done.1) | non-fusion elementwise | flops 917504 | bytes 5505024 | tf_op jit(solution)/shard_map/convert_element_type | solution.py:542
  110.7 22.6 %all_to_all.25 = f16[8,64,1408]{2,1,0:T(8,128)(2,1)S(1)} all-to-all(f16[8,64,1408]{2,1,0:T(8,128)(2,1)S(1)} %bitcast.10), channel_id=1, replica_groups=mesh['x'=4,'zl'=2,'zh'=4,'y'=4,'c'=2] {'x','zl'}, dimensions={0} | all-to-all | bytes 2883584 | tf_op jit(solution)/shard_map/all_to_all | solution.py:55
  133.3 1.8 convert_element_type.18.second
  135.1 5.0 %shard_map.166 = (bf16[8,64,1792]{2,1,0:T(8,128)(2,1)S(1)}, f32[64,384]{1,0:T(8,128)S(1)}, bf16[8,48,896]{2,1,0:T(8,128)(2,1)S(1)}) custom-call(f32[8,64,1792]{2,1,0:T(8,128)} %convert_element_type.16.first, f32[8,64,1408]{2,1,0:T(8,128)} %convert_element_type.18.second, f32[8,48,896]{2,1,0:T(8,128)} %all-to-all-done.b_parts), custom_call_target="tpu_custom_call" | custom-call | flops 176160768 | bytes 6553600 | tf_op jit(solution)/shard_map/pallas_call | solution.py:318
  140.2 1.2 copy-done.3
  142.3 5.9 %all-to-all-start.3 = ((bf16[8,64,1792]{2,1,0:T(8,128)(2,1)}), bf16[8,64,1792]{2,1,0:T(8,128)(2,1)S(1)}, u32[]{:S(2)}, u32[]{:S(2)}) async-start(bf16[8,64,1792]{2,1,0:T(8,128)(2,1)} %copy-done.3), calls=%async_computation.3 | async-start | bytes 3670016 | tf_op jit(solution)/shard_map/all_to_all | solution.py:55
  148.2 1.3 collective-permute-done.17
  149.6 2.0 collective-permute-start.19
  152.3 1.4 copy-done.7
  153.7 4.3 %shard_map.168.selected = bf16[384,512]{1,0:T(8,128)(2,1)S(1)} custom-call(s32[4]{0:T(128)S(1)} %pad_add_fusion.place, bf16[512,1536]{1,0:T(8,128)(2,1)S(1)} %copy-done.5, bf16[512,1536]{1,0:T(8,128)(2,1)S(1)} %copy-done.7), custom_call_target="tpu_custom_call" | custom-call | flops 603979776 | bytes 3145728 | tf_op jit(solution)/shard_map/pallas_call | solution.py:409
  159.5 2.4 %shard_map.167 = bf16[8,112,896]{2,1,0:T(8,128)(2,1)} custom-call(bf16[8,48,896]{2,1,0:T(8,128)(2,1)} %copy-done.10, f32[64,384]{1,0:T(8,128)} %add_add_fusion.g), custom_call_target="tpu_custom_call" | custom-call | tf_op jit(solution)/shard_map/pallas_call | solution.py:387
  161.9 7.5 %all-to-all-done.3 = bf16[8,64,1792]{2,1,0:T(8,128)(2,1)S(1)} async-done(((bf16[8,64,1792]{2,1,0:T(8,128)(2,1)}), bf16[8,64,1792]{2,1,0:T(8,128)(2,1)S(1)}, u32[]{:S(2)}, u32[]{:S(2)}) %all-to-all-start.3) | async-done | bytes 1835040 | tf_op jit(solution)/shard_map/all_to_all | solution.py:55
  169.4 5.6 %all-to-all-start.4 = ((bf16[8,112,896]{2,1,0:T(8,128)(2,1)}), bf16[8,112,896]{2,1,0:T(8,128)(2,1)S(1)}, u32[]{:S(2)}, u32[]{:S(2)}) async-start(bf16[8,112,896]{2,1,0:T(8,128)(2,1)} %shard_map.167), calls=%async_computation.4 | async-start | bytes 3211264 | tf_op jit(solution)/shard_map/all_to_all | solution.py:55
  175.0 1.8 copy-done.1
  176.8 3.6 %shard_map.170 = f32[256,1536]{1,0:T(8,128)S(1)} custom-call(s32[1]{0:T(128)} %bitcast.7.which, bf16[512,1792]{1,0:T(8,128)(2,1)S(1)} %bitcast.8, bf16[1536,896]{1,0:T(8,128)(2,1)S(1)} %copy-done.1, bf16[1536,896]{1,0:T(8,128)(2,1)} %up.3), custom_call_target="tpu_custom_call" | custom-call | flops 1409286144 | bytes 5505024 | tf_op jit(solution)/shard_map/pallas_call | solution.py:343
  180.5 3.6 %shard_map.171.refs_0_ = f32[256,1536]{1,0:T(8,128)S(1)} custom-call(s32[1]{0:T(128)} %bitcast.2.which, bf16[512,1792]{1,0:T(8,128)(2,1)S(1)} %bitcast.9, bf16[1536,896]{1,0:T(8,128)(2,1)S(1)} %copy-done.1, bf16[1536,896]{1,0:T(8,128)(2,1)} %up.3), custom_call_target="tpu_custom_call" | custom-call | flops 1409286144 | bytes 5505024 | tf_op jit(solution)/shard_map/pallas_call | solution.py:343
  185.0 3.2 %collective-permute-start.23 = (bf16[64,1536]{1,0:T(8,128)(2,1)S(1)}, bf16[64,1536]{1,0:T(8,128)(2,1)S(1)}, u32[]{:S(2)}, u32[]{:S(2)}) collective-permute-start(bf16[64,1536]{1,0:T(8,128)(2,1)S(1)} %get-tuple-element.74), channel_id=1, source_target_pairs={{0,6},{2,0},{4,2},{6,4},{1,7},{3,1},{5,3},{7,5},{8,14},{10,8},{12,... | collective-permute-start | bytes 589832 | tf_op jit(solution)/shard_map/ppermute | solution.py:51
  188.2 5.8 %all-to-all-done.4.merged = bf16[8,112,896]{2,1,0:T(8,128)(2,1)S(1)} async-done(((bf16[8,112,896]{2,1,0:T(8,128)(2,1)}), bf16[8,112,896]{2,1,0:T(8,128)(2,1)S(1)}, u32[]{:S(2)}, u32[]{:S(2)}) %all-to-all-start.4) | async-done | bytes 1605664 | tf_op jit(solution)/shard_map/all_to_all | solution.py:55
  194.0 1.7 copy-done.2
  195.6 1.5 shard_map.169
  198.1 2.9 %collective-permute-start.25 = (f32[16,2688]{1,0:T(8,128)S(1)}, f32[16,2688]{1,0:T(8,128)S(1)}, u32[]{:S(2)}, u32[]{:S(2)}) collective-permute-start(f32[16,2688]{1,0:T(8,128)S(1)} %get-tuple-element.78), channel_id=1, source_target_pairs={{0,8},{8,16},{16,24},{24,0},{1,9},{9,17},{17,25},{25,1},{2,10},{10... | collective-permute-start | bytes 516104 | tf_op jit(solution)/shard_map/ppermute | solution.py:51
  201.0 1.6 collective-permute-start.26
  202.5 5.7 %collective-permute-start.27 = (f32[16,2688]{1,0:T(8,128)S(1)}, f32[16,2688]{1,0:T(8,128)S(1)}, u32[]{:S(2)}, u32[]{:S(2)}) collective-permute-start(f32[16,2688]{1,0:T(8,128)S(1)} %get-tuple-element.80), channel_id=1, source_target_pairs={{0,16},{8,24},{16,0},{24,8},{1,17},{9,25},{17,1},{25,9},{2,18},{10... | collective-permute-start | bytes 516104 | tf_op jit(solution)/shard_map/ppermute | solution.py:51
  208.9 3.9 %collective-permute-done.25.refs_1_ = f32[16,2688]{1,0:T(8,128)S(1)} collective-permute-done((f32[16,2688]{1,0:T(8,128)S(1)}, f32[16,2688]{1,0:T(8,128)S(1)}, u32[]{:S(2)}, u32[]{:S(2)}) %collective-permute-start.25) | collective-permute-done | bytes 172064 | tf_op jit(solution)/shard_map/ppermute | solution.py:51
  212.9 8.3 %collective-permute-done.27.refs_3_ = f32[16,2688]{1,0:T(8,128)S(1)} collective-permute-done((f32[16,2688]{1,0:T(8,128)S(1)}, f32[16,2688]{1,0:T(8,128)S(1)}, u32[]{:S(2)}, u32[]{:S(2)}) %collective-permute-start.27) | collective-permute-done | bytes 172064 | tf_op jit(solution)/shard_map/ppermute | solution.py:51
  221.9 1.8 shard_map.174
  (91 shorter events, 17.6 us)
Async XLA Ops:
  2.2 14.5 %collective-permute-start = (bf16[16,5376]{1,0:T(8,128)(2,1)}, bf16[16,5376]{1,0:T(8,128)(2,1)S(1)}, u32[]{:S(2)}, u32[]{:S(2)}) collective-permute-start(bf16[16,5376]{1,0:T(8,128)(2,1)} %shard_map.162.refs_0_), channel_id=1, source_target_pairs={{0,24},{8,0},{16,8},{24,16},{1,25},{9,1},{17,9},{25,17},{2,26},{10... | collective-permute-start | bytes 516104 | tf_op jit(solution)/shard_map/ppermute | solution.py:47
  7.6 16.8 %collective-permute-start.1 = (bf16[16,5376]{1,0:T(8,128)(2,1)}, bf16[16,5376]{1,0:T(8,128)(2,1)S(1)}, u32[]{:S(2)}, u32[]{:S(2)}) collective-permute-start(bf16[16,5376]{1,0:T(8,128)(2,1)} %shard_map.162.refs_0_), channel_id=1, source_target_pairs={{0,16},{8,24},{16,0},{24,8},{1,17},{9,25},{17,1},{25,9},{2,18},{10... | collective-permute-start | bytes 516104 | tf_op jit(solution)/shard_map/ppermute | solution.py:47
  9.0 15.9 %collective-permute-start.2 = (bf16[16,5376]{1,0:T(8,128)(2,1)}, bf16[16,5376]{1,0:T(8,128)(2,1)S(1)}, u32[]{:S(2)}, u32[]{:S(2)}) collective-permute-start(bf16[16,5376]{1,0:T(8,128)(2,1)} %shard_map.162.refs_0_), channel_id=1, source_target_pairs={{0,8},{8,16},{16,24},{24,0},{1,9},{9,17},{17,25},{25,1},{2,10},{10... | collective-permute-start | bytes 516104 | tf_op jit(solution)/shard_map/ppermute | solution.py:47
  16.6 8.3 %copy-start.21 = (bf16[16,5376]{1,0:T(8,128)(2,1)}, bf16[16,5376]{1,0:T(8,128)(2,1)S(1)}, u32[]{:S(2)}) copy-start(bf16[16,5376]{1,0:T(8,128)(2,1)S(1)} %collective-permute-done.refs_1_) | copy-start | bytes 516100
  27.7 7.2 %copy-start.17 = (bf16[64,1536]{1,0:T(8,128)(2,1)S(1)}, bf16[64,1536]{1,0:T(8,128)(2,1)}, u32[]{:S(2)}) copy-start(bf16[64,1536]{1,0:T(8,128)(2,1)} %get-tuple-element.46.refs_0_) | copy-start | bytes 589828
  27.7 19.8 %copy-start.12 = (bf16[64,3840]{1,0:T(8,128)(2,1)S(1)}, bf16[64,3840]{1,0:T(8,128)(2,1)}, u32[]{:S(2)}) copy-start(bf16[64,3840]{1,0:T(8,128)(2,1)} %get-tuple-element.52.refs_0_) | copy-start | bytes 1474564
  28.9 22.4 %copy-start = (bf16[1536,896]{1,0:T(8,128)(2,1)S(1)}, bf16[1536,896]{1,0:T(8,128)(2,1)}, u32[]{:S(2)}) copy-start(bf16[1536,896]{1,0:T(8,128)(2,1)} %gate.3) | copy-start | bytes 8257540
  28.9 46.3 %all-to-all-start = ((f32[8,48,896]{2,1,0:T(8,128)}), f32[8,48,896]{2,1,0:T(8,128)}, u32[]{:S(2)}, u32[]{:S(2)}) async-start(f32[8,48,896]{2,1,0:T(8,128)} %broadcast_in_dim.2), calls=%async_computation | async-start | bytes 2752512 | tf_op jit(solution)/shard_map/all_to_all | solution.py:55
  34.9 9.4 %collective-permute-start.4 = (bf16[64,1536]{1,0:T(8,128)(2,1)S(1)}, bf16[64,1536]{1,0:T(8,128)(2,1)}, u32[]{:S(2)}, u32[]{:S(2)}) collective-permute-start(bf16[64,1536]{1,0:T(8,128)(2,1)S(1)} %copy-done.17), channel_id=1, source_target_pairs={{0,4},{2,6},{4,0},{6,2},{1,5},{3,7},{5,1},{7,3},{8,12},{10,14},{12... | collective-permute-start | bytes 589832 | tf_op jit(solution)/shard_map/ppermute | solution.py:47
  38.1 8.8 %collective-permute-start.3 = (bf16[64,1536]{1,0:T(8,128)(2,1)S(1)}, bf16[64,1536]{1,0:T(8,128)(2,1)}, u32[]{:S(2)}, u32[]{:S(2)}) collective-permute-start(bf16[64,1536]{1,0:T(8,128)(2,1)S(1)} %copy-done.17), channel_id=1, source_target_pairs={{0,6},{2,0},{4,2},{6,4},{1,7},{3,1},{5,3},{7,5},{8,14},{10,8},{12,... | collective-permute-start | bytes 589832 | tf_op jit(solution)/shard_map/ppermute | solution.py:47
  39.1 8.0 %collective-permute-start.5 = (bf16[64,1536]{1,0:T(8,128)(2,1)S(1)}, bf16[64,1536]{1,0:T(8,128)(2,1)}, u32[]{:S(2)}, u32[]{:S(2)}) collective-permute-start(bf16[64,1536]{1,0:T(8,128)(2,1)S(1)} %copy-done.17), channel_id=1, source_target_pairs={{0,2},{2,4},{4,6},{6,0},{1,3},{3,5},{5,7},{7,1},{8,10},{10,12},{12... | collective-permute-start | bytes 589832 | tf_op jit(solution)/shard_map/ppermute | solution.py:47
  40.1 10.1 %collective-permute-start.6 = (bf16[64,1536]{1,0:T(8,128)(2,1)S(1)}, bf16[64,1536]{1,0:T(8,128)(2,1)}, u32[]{:S(2)}, u32[]{:S(2)}) collective-permute-start(bf16[64,1536]{1,0:T(8,128)(2,1)S(1)} %copy-done.17), channel_id=1, source_target_pairs={{0,1},{1,0},{2,3},{3,2},{4,5},{5,4},{6,7},{7,6},{8,9},{9,8},{10,11... | collective-permute-start | bytes 589832 | tf_op jit(solution)/shard_map/ppermute | solution.py:47
  44.3 6.5 %collective-permute-start.8 = (bf16[64,1536]{1,0:T(8,128)(2,1)}, bf16[64,1536]{1,0:T(8,128)(2,1)}, u32[]{:S(2)}, u32[]{:S(2)}) collective-permute-start(bf16[64,1536]{1,0:T(8,128)(2,1)} %collective-permute-done.4.refs_2_), channel_id=1, source_target_pairs={{0,1},{1,0},{2,3},{3,2},{4,5},{5,4},{6,7},{7,6},{8,9},{9,8},{10,11... | collective-permute-start | bytes 589832 | tf_op jit(solution)/shard_map/ppermute | solution.py:47
  46.9 4.4 %collective-permute-start.7 = (bf16[64,1536]{1,0:T(8,128)(2,1)}, bf16[64,1536]{1,0:T(8,128)(2,1)}, u32[]{:S(2)}, u32[]{:S(2)}) collective-permute-start(bf16[64,1536]{1,0:T(8,128)(2,1)} %collective-permute-done.3.refs_1_), channel_id=1, source_target_pairs={{0,1},{1,0},{2,3},{3,2},{4,5},{5,4},{6,7},{7,6},{8,9},{9,8},{10,11... | collective-permute-start | bytes 589832 | tf_op jit(solution)/shard_map/ppermute | solution.py:47
  47.1 4.1 %collective-permute-start.9 = (bf16[64,1536]{1,0:T(8,128)(2,1)}, bf16[64,1536]{1,0:T(8,128)(2,1)}, u32[]{:S(2)}, u32[]{:S(2)}) collective-permute-start(bf16[64,1536]{1,0:T(8,128)(2,1)} %collective-permute-done.5.refs_3_), channel_id=1, source_target_pairs={{0,1},{1,0},{2,3},{3,2},{4,5},{5,4},{6,7},{7,6},{8,9},{9,8},{10,11... | collective-permute-start | bytes 589832 | tf_op jit(solution)/shard_map/ppermute | solution.py:47
  47.5 23.9 %collective-permute-start.10 = (bf16[64,3840]{1,0:T(8,128)(2,1)S(1)}, bf16[64,3840]{1,0:T(8,128)(2,1)S(1)}, u32[]{:S(2)}, u32[]{:S(2)}) collective-permute-start(bf16[64,3840]{1,0:T(8,128)(2,1)S(1)} %copy-done.12), channel_id=1, source_target_pairs={{0,6},{2,0},{4,2},{6,4},{1,7},{3,1},{5,3},{7,5},{8,14},{10,8},{12,... | collective-permute-start | bytes 1474568 | tf_op jit(solution)/shard_map/ppermute | solution.py:47
  50.2 21.2 %collective-permute-start.11 = (bf16[64,3840]{1,0:T(8,128)(2,1)S(1)}, bf16[64,3840]{1,0:T(8,128)(2,1)S(1)}, u32[]{:S(2)}, u32[]{:S(2)}) collective-permute-start(bf16[64,3840]{1,0:T(8,128)(2,1)S(1)} %copy-done.12), channel_id=1, source_target_pairs={{0,4},{2,6},{4,0},{6,2},{1,5},{3,7},{5,1},{7,3},{8,12},{10,14},{12... | collective-permute-start | bytes 1474568 | tf_op jit(solution)/shard_map/ppermute | solution.py:47
  50.8 24.4 %collective-permute-start.12 = (bf16[64,3840]{1,0:T(8,128)(2,1)S(1)}, bf16[64,3840]{1,0:T(8,128)(2,1)}, u32[]{:S(2)}, u32[]{:S(2)}) collective-permute-start(bf16[64,3840]{1,0:T(8,128)(2,1)S(1)} %copy-done.12), channel_id=1, source_target_pairs={{0,2},{2,4},{4,6},{6,0},{1,3},{3,5},{5,7},{7,1},{8,10},{10,12},{12... | collective-permute-start | bytes 1474568 | tf_op jit(solution)/shard_map/ppermute | solution.py:47
  78.7 5.8 %copy-start.14 = (bf16[64,3840]{1,0:T(8,128)(2,1)S(1)}, bf16[64,3840]{1,0:T(8,128)(2,1)}, u32[]{:S(2)}) copy-start(bf16[64,3840]{1,0:T(8,128)(2,1)} %copy-done.13) | copy-start | bytes 1474564
  78.7 6.4 %copy-start.16 = (bf16[64,3840]{1,0:T(8,128)(2,1)S(1)}, bf16[64,3840]{1,0:T(8,128)(2,1)}, u32[]{:S(2)}) copy-start(bf16[64,3840]{1,0:T(8,128)(2,1)} %copy-done.15) | copy-start | bytes 1474564
  78.7 28.2 %all-to-all-start.1 = ((f16[8,64,1792]{2,1,0:T(8,128)(2,1)}), f16[8,64,1792]{2,1,0:T(8,128)(2,1)}, u32[]{:S(2)}, u32[]{:S(2)}) async-start(f16[8,64,1792]{2,1,0:T(8,128)(2,1)} %bitcast.4), calls=%async_computation.1 | async-start | bytes 3670016 | tf_op jit(solution)/shard_map/all_to_all | solution.py:55
  84.6 1.9 collective-permute-start.13
  84.6 3.3 %collective-permute-start.14 = (bf16[64,3840]{1,0:T(8,128)(2,1)S(1)}, bf16[64,3840]{1,0:T(8,128)(2,1)S(1)}, u32[]{:S(2)}, u32[]{:S(2)}) collective-permute-start(bf16[64,3840]{1,0:T(8,128)(2,1)S(1)} %copy-done.14), channel_id=1, source_target_pairs={{0,1},{1,0},{2,3},{3,2},{4,5},{5,4},{6,7},{7,6},{8,9},{9,8},{10,11... | collective-permute-start | bytes 1474568 | tf_op jit(solution)/shard_map/ppermute | solution.py:47
  85.1 3.5 %collective-permute-start.15 = (bf16[64,3840]{1,0:T(8,128)(2,1)S(1)}, bf16[64,3840]{1,0:T(8,128)(2,1)S(1)}, u32[]{:S(2)}, u32[]{:S(2)}) collective-permute-start(bf16[64,3840]{1,0:T(8,128)(2,1)S(1)} %copy-done.16), channel_id=1, source_target_pairs={{0,1},{1,0},{2,3},{3,2},{4,5},{5,4},{6,7},{7,6},{8,9},{9,8},{10,11... | collective-permute-start | bytes 1474568 | tf_op jit(solution)/shard_map/ppermute | solution.py:47
  85.2 3.4 %collective-permute-start.16 = (bf16[64,3840]{1,0:T(8,128)(2,1)}, bf16[64,3840]{1,0:T(8,128)(2,1)S(1)}, u32[]{:S(2)}, u32[]{:S(2)}) collective-permute-start(bf16[64,3840]{1,0:T(8,128)(2,1)} %collective-permute-done.12.refs_3_), channel_id=1, source_target_pairs={{0,1},{1,0},{2,3},{3,2},{4,5},{5,4},{6,7},{7,6},{8,9},{9,8},{10,11... | collective-permute-start | bytes 1474568 | tf_op jit(solution)/shard_map/ppermute | solution.py:47
  100.3 10.2 %copy-start.18 = (f32[512,1408]{1,0:T(8,128)S(1)}, f32[512,1408]{1,0:T(8,128)}, u32[]{:S(2)}) copy-start(f32[512,1408]{1,0:T(8,128)} %get-tuple-element.60) | copy-start | bytes 8650756
  140.2 1.2 copy-start.3
  142.3 10.1 %copy-start.5 = (bf16[512,1536]{1,0:T(8,128)(2,1)S(1)}, bf16[512,1536]{1,0:T(8,128)(2,1)}, u32[]{:S(2)}) copy-start(bf16[512,1536]{1,0:T(8,128)(2,1)} %copy-done.4) | copy-start | bytes 4718596
  142.3 27.1 %all-to-all-start.3 = ((bf16[8,64,1792]{2,1,0:T(8,128)(2,1)}), bf16[8,64,1792]{2,1,0:T(8,128)(2,1)S(1)}, u32[]{:S(2)}, u32[]{:S(2)}) async-start(bf16[8,64,1792]{2,1,0:T(8,128)(2,1)} %copy-done.3), calls=%async_computation.3 | async-start | bytes 3670016 | tf_op jit(solution)/shard_map/all_to_all | solution.py:55
  148.2 1.3 collective-permute-start.17
  149.5 9.3 %collective-permute-start.18 = (f32[64,384]{1,0:T(8,128)S(1)}, f32[64,384]{1,0:T(8,128)S(1)}, u32[]{:S(2)}, u32[]{:S(2)}) collective-permute-start(f32[64,384]{1,0:T(8,128)S(1)} %add.23), channel_id=1, source_target_pairs={{0,6},{2,0},{4,2},{6,4},{1,7},{3,1},{5,3},{7,5},{8,14},{10,8},{12,... | collective-permute-start | bytes 294920 | tf_op jit(solution)/shard_map/ppermute | solution.py:47
  149.6 9.3 %collective-permute-start.19 = (f32[64,384]{1,0:T(8,128)S(1)}, f32[64,384]{1,0:T(8,128)S(1)}, u32[]{:S(2)}, u32[]{:S(2)}) collective-permute-start(f32[64,384]{1,0:T(8,128)S(1)} %add.23), channel_id=1, source_target_pairs={{0,2},{2,4},{4,6},{6,0},{1,3},{3,5},{5,7},{7,1},{8,10},{10,12},{12... | collective-permute-start | bytes 294920 | tf_op jit(solution)/shard_map/ppermute | solution.py:47
  151.6 7.2 %collective-permute-start.20 = (f32[64,384]{1,0:T(8,128)S(1)}, f32[64,384]{1,0:T(8,128)S(1)}, u32[]{:S(2)}, u32[]{:S(2)}) collective-permute-start(f32[64,384]{1,0:T(8,128)S(1)} %add.23), channel_id=1, source_target_pairs={{0,4},{2,6},{4,0},{6,2},{1,5},{3,7},{5,1},{7,3},{8,12},{10,14},{12... | collective-permute-start | bytes 294920 | tf_op jit(solution)/shard_map/ppermute | solution.py:47
  152.3 1.4 copy-start.7
  169.4 24.6 %all-to-all-start.4 = ((bf16[8,112,896]{2,1,0:T(8,128)(2,1)}), bf16[8,112,896]{2,1,0:T(8,128)(2,1)S(1)}, u32[]{:S(2)}, u32[]{:S(2)}) async-start(bf16[8,112,896]{2,1,0:T(8,128)(2,1)} %shard_map.167), calls=%async_computation.4 | async-start | bytes 3211264 | tf_op jit(solution)/shard_map/all_to_all | solution.py:55
  175.0 1.8 copy-start.1
  180.4 3.7 %collective-permute-start.21 = (f32[256,1536]{1,0:T(8,128)S(1)}, f32[256,1536]{1,0:T(8,128)S(1)}, u32[]{:S(2)}, u32[]{:S(2)}) collective-permute-start(f32[256,1536]{1,0:T(8,128)S(1)} %shard_map.170), channel_id=1, source_target_pairs={{0,1},{1,0},{2,3},{3,2},{4,5},{5,4},{6,7},{7,6},{8,9},{9,8},{10,11... | collective-permute-start | bytes 4718600 | tf_op jit(solution)/shard_map/ppermute | solution.py:47
  184.1 9.9 %copy-start.9 = (bf16[384,512]{1,0:T(8,128)(2,1)S(1)}, bf16[384,512]{1,0:T(8,128)(2,1)}, u32[]{:S(2)}) copy-start(bf16[384,512]{1,0:T(8,128)(2,1)} %copy-done.8) | copy-start | bytes 1179652
  185.0 12.9 %collective-permute-start.22 = (bf16[64,1536]{1,0:T(8,128)(2,1)}, bf16[64,1536]{1,0:T(8,128)(2,1)S(1)}, u32[]{:S(2)}, u32[]{:S(2)}) collective-permute-start(bf16[64,1536]{1,0:T(8,128)(2,1)} %get-tuple-element.73), channel_id=1, source_target_pairs={{0,2},{2,4},{4,6},{6,0},{1,3},{3,5},{5,7},{7,1},{8,10},{10,12},{12... | collective-permute-start | bytes 589832 | tf_op jit(solution)/shard_map/ppermute | solution.py:51
  185.0 12.9 %collective-permute-start.23 = (bf16[64,1536]{1,0:T(8,128)(2,1)S(1)}, bf16[64,1536]{1,0:T(8,128)(2,1)S(1)}, u32[]{:S(2)}, u32[]{:S(2)}) collective-permute-start(bf16[64,1536]{1,0:T(8,128)(2,1)S(1)} %get-tuple-element.74), channel_id=1, source_target_pairs={{0,6},{2,0},{4,2},{6,4},{1,7},{3,1},{5,3},{7,5},{8,14},{10,8},{12,... | collective-permute-start | bytes 589832 | tf_op jit(solution)/shard_map/ppermute | solution.py:51
  188.2 9.7 %collective-permute-start.24 = (bf16[64,1536]{1,0:T(8,128)(2,1)S(1)}, bf16[64,1536]{1,0:T(8,128)(2,1)S(1)}, u32[]{:S(2)}, u32[]{:S(2)}) collective-permute-start(bf16[64,1536]{1,0:T(8,128)(2,1)S(1)} %get-tuple-element.75), channel_id=1, source_target_pairs={{0,4},{2,6},{4,0},{6,2},{1,5},{3,7},{5,1},{7,3},{8,12},{10,14},{12... | collective-permute-start | bytes 589832 | tf_op jit(solution)/shard_map/ppermute | solution.py:51
  194.0 1.7 copy-start.2
  198.0 23.2 %copy-start.11 = (f32[16,2688]{1,0:T(8,128)}, f32[16,2688]{1,0:T(8,128)S(1)}, u32[]{:S(2)}) copy-start(f32[16,2688]{1,0:T(8,128)S(1)} %get-tuple-element.77.refs_0_) | copy-start | bytes 516100
  198.1 14.8 %collective-permute-start.25 = (f32[16,2688]{1,0:T(8,128)S(1)}, f32[16,2688]{1,0:T(8,128)S(1)}, u32[]{:S(2)}, u32[]{:S(2)}) collective-permute-start(f32[16,2688]{1,0:T(8,128)S(1)} %get-tuple-element.78), channel_id=1, source_target_pairs={{0,8},{8,16},{16,24},{24,0},{1,9},{9,17},{17,25},{25,1},{2,10},{10... | collective-permute-start | bytes 516104 | tf_op jit(solution)/shard_map/ppermute | solution.py:51
  201.0 11.9 %collective-permute-start.26 = (f32[16,2688]{1,0:T(8,128)S(1)}, f32[16,2688]{1,0:T(8,128)S(1)}, u32[]{:S(2)}, u32[]{:S(2)}) collective-permute-start(f32[16,2688]{1,0:T(8,128)S(1)} %get-tuple-element.79), channel_id=1, source_target_pairs={{0,24},{8,0},{16,8},{24,16},{1,25},{9,1},{17,9},{25,17},{2,26},{10... | collective-permute-start | bytes 516104 | tf_op jit(solution)/shard_map/ppermute | solution.py:51
  202.5 18.7 %collective-permute-start.27 = (f32[16,2688]{1,0:T(8,128)S(1)}, f32[16,2688]{1,0:T(8,128)S(1)}, u32[]{:S(2)}, u32[]{:S(2)}) collective-permute-start(f32[16,2688]{1,0:T(8,128)S(1)} %get-tuple-element.80), channel_id=1, source_target_pairs={{0,16},{8,24},{16,0},{24,8},{1,17},{9,25},{17,1},{25,9},{2,18},{10... | collective-permute-start | bytes 516104 | tf_op jit(solution)/shard_map/ppermute | solution.py:51
  212.9 8.3 %copy-start.19 = (f32[16,2688]{1,0:T(8,128)}, f32[16,2688]{1,0:T(8,128)S(1)}, u32[]{:S(2)}) copy-start(f32[16,2688]{1,0:T(8,128)S(1)} %collective-permute-done.25.refs_1_) | copy-start | bytes 516100
  212.9 8.3 %copy-start.20 = (f32[16,2688]{1,0:T(8,128)}, f32[16,2688]{1,0:T(8,128)S(1)}, u32[]{:S(2)}) copy-start(f32[16,2688]{1,0:T(8,128)S(1)} %collective-permute-done.26.refs_2_) | copy-start | bytes 516100
  (9 other events, 7.5 us)

commit v2 on v1

--- a/solution.py
+++ b/solution.py
@@ -16,7 +16,8 @@
 VMEM = pl.BlockSpec(memory_space=pltpu.VMEM)
 SMEM = pl.BlockSpec(memory_space=pltpu.SMEM)
 ANY = pl.BlockSpec(memory_space=pl.ANY)
-PARAMS = pltpu.CompilerParams(vmem_limit_bytes=48 * 1024 * 1024)
+PARAMS = pltpu.CompilerParams(vmem_limit_bytes=28 * 1024 * 1024)
+LARGE = pltpu.CompilerParams(vmem_limit_bytes=60 * 1024 * 1024)
 
 
 def split(a):
@@ -147,36 +148,16 @@
 
     def kernel(place, *refs):
         piece = refs[:8]
-        gate, up, part_out, x_out, exponents_out = refs[8:13]
-        part, x, w_gate, w_up, sem_x, sem_w, sem_o = refs[13:]
-        moves = panel_moves(place, piece, 0, width, x, sem_x)
-        load = [
-            pltpu.make_async_copy(a, b, sem_w.at[i])
-            for i, (a, b) in enumerate(((gate, w_gate), (up, w_up)))
-        ]
-        store = [
-            pltpu.make_async_copy(
-                part.at[:, pl.ds(i * units, units)],
-                part_out.at[:, pl.ds(i * units, units)],
-                sem_o.at[i],
-            )
-            for i in range(2)
-        ]
-        store_x = pltpu.make_async_copy(x, x_out, sem_o.at[2])
-        for copy in moves + load:
-            copy.start()
-        for copy in moves + load[:1]:
-            copy.wait()
-        store_x.start()
+        gate, up, part, x, exponents_out, sem = refs[8:]
+        moves = panel_moves(place, piece, 0, width, x, sem)
+        for move in moves:
+            move.start()
+        for move in moves:
+            move.wait()
         exponents = jnp.zeros((1, 128), F32)
-        exponents = scaled(part, 0, units, lambda at: dot(x[at, :], w_gate[...]), 0, exponents)
-        store[0].start()
-        load[1].wait()
-        exponents = scaled(part, units, units, lambda at: dot(x[at, :], w_up[...]), 1, exponents)
-        store[1].start()
+        exponents = scaled(part, 0, units, lambda at: dot(x[at, :], gate[...]), 0, exponents)
+        exponents = scaled(part, units, units, lambda at: dot(x[at, :], up[...]), 1, exponents)
         exponents_out[...] = jnp.broadcast_to(exponents, (8, 128))
-        for copy in store + [store_x]:
-            copy.wait()
 
     return pl.pallas_call(
         kernel,
@@ -185,19 +166,11 @@
             shape((rows, width), BF16),
             shape((8, 128), F32),
         ),
-        in_specs=[SMEM] + [ANY] * 10,
-        out_specs=(ANY, ANY, VMEM),
-        scratch_shapes=[
-            pltpu.VMEM((rows, 2 * units), F32),
-            pltpu.VMEM((rows, width), BF16),
-            pltpu.VMEM(gate_w.shape, BF16),
-            pltpu.VMEM(up_w.shape, BF16),
-            pltpu.SemaphoreType.DMA((8,)),
-            pltpu.SemaphoreType.DMA((2,)),
-            pltpu.SemaphoreType.DMA((3,)),
-        ],
-        compiler_params=PARAMS,
-        cost_estimate=cost(12 * rows * width * units, gate_w, up_w),
+        in_specs=[SMEM] + [VMEM] * 10,
+        out_specs=(VMEM, VMEM, VMEM),
+        scratch_shapes=[pltpu.SemaphoreType.DMA((8,))],
+        compiler_params=PARAMS,
+        cost_estimate=cost(33 * rows * width * units, gate_w, up_w),
     )(place, *pieces, gate_w, up_w)
 
 
@@ -211,26 +184,19 @@
 
     def kernel(place, *refs):
         piece = refs[:8]
-        x_in, down, exponents_in, part, dy_out, factors = refs[8:14]
-        x, dy, packed, w_down, sem_dy, sem_a, sem_w, sem_o = refs[14:]
+        x, down, exponents_in, part, dy, factors, packed, sem_dy, sem_a = refs[8:]
         move_dy = panel_moves(place, piece, 0, width, dy, sem_dy)
         move_a = panel_moves(place, piece, width, lanes - width, packed, sem_a)
-        load = [
-            pltpu.make_async_copy(down, w_down, sem_w.at[0]),
-            pltpu.make_async_copy(x_in, x, sem_w.at[1]),
-        ]
-        store_dy = pltpu.make_async_copy(dy, dy_out, sem_o)
-        for copy in move_dy + load[:1] + move_a + load[1:]:
-            copy.start()
-        for copy in move_dy + load[:1]:
-            copy.wait()
-        store_dy.start()
+        for move in move_dy + move_a:
+            move.start()
+        for move in move_dy:
+            move.wait()
         exponents = exponents_in[0:1, :]
         exponents = scaled(
-            part, 0, units, lambda at: dot(dy[at, :], w_down[...], ((1,), (1,))), 2, exponents
+            part, 0, units, lambda at: dot(dy[at, :], down[...], ((1,), (1,))), 2, exponents
         )
-        for copy in move_a + load[1:]:
-            copy.wait()
+        for move in move_a:
+            move.wait()
         for c in range(NC):
             for y in range(NY):
                 for zh in range(NZH):
@@ -249,7 +215,6 @@
                 part, units + i * rank, rank, lambda at: value[at, :], 3 + i, exponents
             )
         part[:, units + ranks :] = jnp.broadcast_to(exponents, (rows, 128))
-        store_dy.wait()
 
     return pl.pallas_call(
         kernel,
@@ -258,20 +223,15 @@
             shape((rows, width), BF16),
             shape((width, 2 * ranks), BF16),
         ),
-        in_specs=[SMEM] + [ANY] * 10 + [VMEM],
-        out_specs=(VMEM, ANY, VMEM),
+        in_specs=[SMEM] + [VMEM] * 11,
+        out_specs=(VMEM, VMEM, VMEM),
         scratch_shapes=[
-            pltpu.VMEM((rows, width), BF16),
-            pltpu.VMEM((rows, width), BF16),
             pltpu.VMEM((rows, lanes - width), BF16),
-            pltpu.VMEM(down_w.shape, BF16),
             pltpu.SemaphoreType.DMA((8,)),
             pltpu.SemaphoreType.DMA((8,)),
-            pltpu.SemaphoreType.DMA((2,)),
-            pltpu.SemaphoreType.DMA,
         ],
         compiler_params=PARAMS,
-        cost_estimate=cost(12 * rows * width * units, down_w, x),
+        cost_estimate=cost(38 * rows * width * units, down_w, x),
     )(place, *pieces, x, down_w, exponents)
 
 
@@ -320,7 +280,7 @@
         out_shape=(
             shape((NROW, per, 2 * units), BF16),
             shape((per, ranks), F32),
-            shape(b_parts.shape, BF16),
+            shape((NROW, 3 * share, units), BF16),
         ),
         in_specs=[VMEM] * 3,
         out_specs=(VMEM,) * 3,
@@ -454,37 +414,44 @@
     features = grads.shape[0] // NZH
     ranks = grads.shape[1]
     groups = features // block
+    lanes = width + groups * ranks
 
     def kernel(here, grads, *refs):
-        ins, outs = refs[: len(parts)], refs[len(parts) :]
-        for s, out in zip((0,) + SHIFTS, outs):
-            to = lax.rem(here[0] + s, NZH)
+        ins, (own, wide) = refs[: len(parts)], refs[len(parts) :]
+
+        def fill(to, out):
             at = pl.ds(pl.multiple_of(to * block, block), block)
             total = ins[0][at, :].astype(F32)
             for ref in ins[1:]:
                 total = total + ref[at, :].astype(F32)
-            out[:, :width] = total
+            out[:, :width] = total.astype(out.dtype)
             for k in range(groups):
                 at = pl.ds(pl.multiple_of(to * features + k * block, block), block)
-                out[:, width + k * ranks : width + (k + 1) * ranks] = grads[at, :]
-
-    return pl.pallas_call(
-        kernel,
-        out_shape=(shape((block, width + groups * ranks), F32),) * 4,
+                out[:, width + k * ranks : width + (k + 1) * ranks] = grads[at, :].astype(out.dtype)
+
+        fill(here[0], own)
+        for zh in range(NZH):
+            fill(zh, wide.at[zh])
+        wide[here[0]] = jnp.zeros((block, lanes), wide.dtype)
+
+    return pl.pallas_call(
+        kernel,
+        out_shape=(shape((block, lanes), F32), shape((NZH, block, lanes), BF16)),
         in_specs=[SMEM] + [VMEM] * (1 + len(parts)),
-        out_specs=(VMEM,) * 4,
+        out_specs=(VMEM,) * 2,
         compiler_params=PARAMS,
     )(here, grads, *parts)
 
 
-def finish(width, rank, *parts):
-    own, lanes = parts[0].shape
+def finish(width, rank, kept, others):
+    own, lanes = kept.shape
     ranks = 3 * rank
     groups = (lanes - width) // ranks
 
-    def kernel(*refs):
-        ins, (tokens, *factors) = refs[:4], refs[4:]
-        total = (ins[0][...] + ins[1][...]) + (ins[2][...] + ins[3][...])
+    def kernel(kept, others, tokens, *factors):
+        total = kept[...]
+        for zh in range(NZH):
+            total = total + others[zh].astype(F32)
         tokens[...] = total[:, :width]
         for k in range(groups):
             for i, out in enumerate(factors):
@@ -494,9 +461,9 @@
     return pl.pallas_call(
         kernel,
         out_shape=(shape((own, width), F32),) + (shape((own * groups, rank), F32),) * 3,
-        in_specs=[VMEM] * 4,
+        in_specs=[VMEM] * 2,
         out_specs=(VMEM,) * 4,
-    )(*parts)
+    )(kept, others)
 
 
 def after(value, *others):
@@ -531,26 +498,27 @@
     def with_core(pieces):
         return pieces + [from_next(p, "c", NC, 1) for p in pieces]
 
+    pieces = from_y(near)
+    late_pieces = from_y(after(late, *pieces[1:]))
     b_own = after(jnp.concatenate([gate_b, up_b, down_a_t], axis=0), near)
     b_parts = exchange(jnp.broadcast_to(b_own[None], (NROW,) + b_own.shape), ROW)
-    pieces = from_y(near)
-    late_pieces = from_y(after(late, pieces[2]))
     pieces = with_core(pieces)
 
-    def sums(part):
-        sent = part.astype(F16).reshape(NROW, rows // NROW, part.shape[1])
-        return exchange(sent, ROW).astype(F32)
+    def half(part):
+        return part.astype(F16).reshape(NROW, rows // NROW, part.shape[1])
 
     part_x, x, exponents = forward_x(place, pieces, gate_w, up_w)
     rows = x.shape[0]
-    part_x, b_parts, *late_pieces = lax.optimization_barrier((part_x, b_parts, *late_pieces))
+    part_x, b_parts = lax.optimization_barrier((half(part_x), b_parts))
+    *late_pieces, exponents = lax.optimization_barrier((*late_pieces, exponents))
     part_dy, dy, factors = forward_dy(
         place, with_core(late_pieces), x, down_w, exponents, ranks, own_features
     )
-    sums_x = sums(part_x)
-    sums_x, part_dy = lax.optimization_barrier((sums_x, part_dy))
+    sums_x, part_dy = lax.optimization_barrier((exchange(part_x, ROW), half(part_dy)))
     selected = select(place, x, dy, own_features)
-    wide, g, factor_parts = swiglu_back(sums_x, sums(part_dy), b_parts)
+    wide, g, factor_parts = swiglu_back(
+        sums_x.astype(F32), exchange(part_dy, ROW).astype(F32), b_parts
+    )
 
     d_all = exchange(wide, ROW).reshape(rows, 2 * units)
 
@@ -567,9 +535,10 @@
     others = [to_next(a, "y", NY, s) for s, a in zip(SHIFTS, sends)]
 
     grads, adapter = rank_grads(place, selected, merged, factors, ranks)
-    kept, *sends = cut_last(at_zh, grads, kept, *others, adapter)
-    others = [to_next(a, "zh", NZH, s) for s, a in zip(SHIFTS, sends)]
-    grad_tokens, grad_gate_a, grad_up_a, grad_down_b_t = finish(width, rank, kept, *others)
+    kept, sends = cut_last(at_zh, grads, kept, *others, adapter)
+    grad_tokens, grad_gate_a, grad_up_a, grad_down_b_t = finish(
+        width, rank, kept, exchange(sends, "zh")
+    )
 
     share = gate_b.shape[0]
     factor_grads = merged[:, : 3 * share].astype(F32).sum(0)

time: 225 us -> 196 us (0.87)
  blocking collectives: 22.6 us -> 0 us
  waiting for transfers between devices: 70.1 us -> 57.4 us
  starting transfers between devices: 59.1 us -> 69.1 us
  Pallas kernels: 45.3 us -> 36.7 us
  local copies, waits for them, and re-layouts: 14.8 us -> 21.9 us
  other arithmetic: 10.9 us -> 8.25 us
    all_to_all x1 -> x0, blocking collectives: 22.6 us -> none  [exchange(): return lax.all_to_all(wide, axis, split_axis=0, concat_axis=0)]
    ppermute x22, waiting for transfers between devices: 37.2 us -> 19.7 us  [from_next(): return lax.ppermute(a, axis, [(j, (j - s) % n) for j in range(n)])]
    all_to_all x4 -> x6, waiting for transfers between devices: 19.9 us -> 36.6 us  [exchange(): return lax.all_to_all(wide, axis, split_axis=0, concat_axis=0)]
    all_to_all x4 -> x6, starting transfers between devices: 23.3 us -> 37.6 us  [exchange(): return lax.all_to_all(wide, axis, split_axis=0, concat_axis=0)]
    ppermute x6 -> x3, waiting for transfers between devices: 13 us -> 1.15 us  [to_next(): return lax.ppermute(a, axis, [(j, (j + s) % n) for j in range(n)])]
    ppermute x6 -> x3, starting transfers between devices: 13.4 us -> 4.17 us  [to_next(): return lax.ppermute(a, axis, [(j, (j + s) % n) for j in range(n)])]
    unnamed x50 -> x46, local copies, waits for them, and re-layouts: 13 us -> 20 us
    ppermute x22, starting transfers between devices: 22.4 us -> 27.3 us  [from_next(): return lax.ppermute(a, axis, [(j, (j - s) % n) for j in range(n)])]
  transfers between devices with their start and end apart: 32 -> 31, of which waited for: 18 -> 18; matrix products, arithmetic and copies ran while one was open for 1% -> 5% of each run, Pallas kernels for 16% -> 14%
where the time goes in v2:
time: 196 us; the launch traced here: 194 us
  starting transfers between devices  69.1 us (35%)
  waiting for transfers between devices  57.4 us (29%)
  Pallas kernels  36.7 us (19%)
  local copies, waits for them, and re-layouts  21.9 us (11%)
  other arithmetic  8.25 us (4%)
    all_to_all x6, starting transfers between devices, exchange(): return lax.all_to_all(wide, axis, split_axis=0, concat_axis=0)  37.6 us
    all_to_all x6, waiting for transfers between devices, exchange(): return lax.all_to_all(wide, axis, split_axis=0, concat_axis=0)  36.6 us
    ppermute x22, starting transfers between devices, from_next(): return lax.ppermute(a, axis, [(j, (j - s) % n) for j in range(n)])  27.3 us
    unnamed x46, local copies, waits for them, and re-layouts  20 us
    ppermute x22, waiting for transfers between devices, from_next(): return lax.ppermute(a, axis, [(j, (j - s) % n) for j in range(n)])  19.7 us
    pallas_call x1, Pallas kernels, forward_x(): pl.pallas_call(kernel, out_shape=(shape((rows, 2 * units), F32), shape((r...  7.36 us
    pallas_call x1, Pallas kernels, forward_dy(): pl.pallas_call(kernel, out_shape=(shape((rows, units + ranks + 128), F32)...  7.26 us
    pallas_call x1, Pallas kernels, select(): pl.pallas_call(kernel, out_shape=shape((2 * NZH * own_features, rows), BF...  4.33 us
  transfers between devices with their start and end apart: 31, of which 18 were waited for; matrix products, arithmetic and copies ran while one was open for 5% of the time, Pallas kernels for 14%

profile of v2, /device:TPU:34, one launch (start us, length us, event | category | flops | bytes accessed | tf_op | source)
XLA Modules:
  0.0 194.2 jit_solution(10713396985744096192)
XLA Ops:
  0.6 1.5 shard_map.162.refs_0_
  2.2 3.3 %collective-permute-start.2 = (bf16[16,5376]{1,0:T(8,128)(2,1)}, bf16[16,5376]{1,0:T(8,128)(2,1)S(1)}, u32[]{:S(2)}, u32[]{:S(2)}) collective-permute-start(bf16[16,5376]{1,0:T(8,128)(2,1)} %shard_map.162.refs_0_), channel_id=1, source_target_pairs={{0,8},{8,16},{16,24},{24,0},{1,9},{9,17},{17,25},{25,1},{2,10},{10... | collective-permute-start | bytes 516104 | tf_op jit(solution)/shard_map/ppermute | solution.py:48
  5.4 4.5 %collective-permute-start.1 = (bf16[16,5376]{1,0:T(8,128)(2,1)}, bf16[16,5376]{1,0:T(8,128)(2,1)S(1)}, u32[]{:S(2)}, u32[]{:S(2)}) collective-permute-start(bf16[16,5376]{1,0:T(8,128)(2,1)} %shard_map.162.refs_0_), channel_id=1, source_target_pairs={{0,16},{8,24},{16,0},{24,8},{1,17},{9,25},{17,1},{25,9},{2,18},{10... | collective-permute-start | bytes 516104 | tf_op jit(solution)/shard_map/ppermute | solution.py:48
  9.9 2.7 %collective-permute-start = (bf16[16,5376]{1,0:T(8,128)(2,1)}, bf16[16,5376]{1,0:T(8,128)(2,1)S(1)}, u32[]{:S(2)}, u32[]{:S(2)}) collective-permute-start(bf16[16,5376]{1,0:T(8,128)(2,1)} %shard_map.162.refs_0_), channel_id=1, source_target_pairs={{0,24},{8,0},{16,8},{24,16},{1,25},{9,1},{17,9},{25,17},{2,26},{10... | collective-permute-start | bytes 516104 | tf_op jit(solution)/shard_map/ppermute | solution.py:48
  12.6 6.3 %collective-permute-done.2.refs_3_ = bf16[16,5376]{1,0:T(8,128)(2,1)S(1)} collective-permute-done((bf16[16,5376]{1,0:T(8,128)(2,1)}, bf16[16,5376]{1,0:T(8,128)(2,1)S(1)}, u32[]{:S(2)}, u32[]{:S(2)}) %collective-permute-start.2) | collective-permute-done | bytes 172064 | tf_op jit(solution)/shard_map/ppermute | solution.py:48
  18.9 1.3 collective-permute-done.1.refs_2_
  20.2 2.4 %collective-permute-done.refs_1_ = bf16[16,5376]{1,0:T(8,128)(2,1)S(1)} collective-permute-done((bf16[16,5376]{1,0:T(8,128)(2,1)}, bf16[16,5376]{1,0:T(8,128)(2,1)S(1)}, u32[]{:S(2)}, u32[]{:S(2)}) %collective-permute-start) | collective-permute-done | bytes 172064 | tf_op jit(solution)/shard_map/ppermute | solution.py:48
  23.2 2.1 %shard_map.163 = (bf16[64,1536]{1,0:T(8,128)(2,1)}, bf16[64,3840]{1,0:T(8,128)(2,1)}) custom-call(s32[1]{0:T(128)} %bitcast.here, bf16[16,5376]{1,0:T(8,128)(2,1)} %shard_map.162.refs_0_, bf16[16,5376]{1,0:T(8,128)(2,1)} %copy-done.22, bf16[16,5376]{1,0:T(8,128)(2,1)} %copy-done.21, bf16[16,5376]{1,0:T(8,128)(2,1)} %copy-done.20), custom_call_target="tpu_custom_call" | custom-call | tf_op jit(solution)/shard_map/pallas_call | solution.py:99
  25.3 1.6 collective-permute-start.5
  26.9 2.9 %collective-permute-start.4 = (bf16[64,1536]{1,0:T(8,128)(2,1)}, bf16[64,1536]{1,0:T(8,128)(2,1)}, u32[]{:S(2)}, u32[]{:S(2)}) collective-permute-start(bf16[64,1536]{1,0:T(8,128)(2,1)} %get-tuple-element.45.refs_0_), channel_id=1, source_target_pairs={{0,4},{2,6},{4,0},{6,2},{1,5},{3,7},{5,1},{7,3},{8,12},{10,14},{12... | collective-permute-start | bytes 589832 | tf_op jit(solution)/shard_map/ppermute | solution.py:48
  29.8 1.3 collective-permute-start.3
  33.2 8.7 %all-to-all-start = ((f32[8,48,896]{2,1,0:T(8,128)}), f32[8,48,896]{2,1,0:T(8,128)}, u32[]{:S(2)}, u32[]{:S(2)}) async-start(f32[8,48,896]{2,1,0:T(8,128)} %broadcast_in_dim.2), calls=%async_computation | async-start | bytes 2752512 | tf_op jit(solution)/shard_map/all_to_all | solution.py:56
  44.6 2.3 %collective-permute-start.10 = (bf16[64,3840]{1,0:T(8,128)(2,1)S(1)}, bf16[64,3840]{1,0:T(8,128)(2,1)}, u32[]{:S(2)}, u32[]{:S(2)}) collective-permute-start(bf16[64,3840]{1,0:T(8,128)(2,1)S(1)} %copy-done.17), channel_id=1, source_target_pairs={{0,6},{2,0},{4,2},{6,4},{1,7},{3,1},{5,3},{7,5},{8,14},{10,8},{12,... | collective-permute-start | bytes 1474568 | tf_op jit(solution)/shard_map/ppermute | solution.py:48
  46.9 1.8 copy-done.3
  48.7 7.4 %shard_map.164 = (f32[512,1792]{1,0:T(8,128)S(1)}, bf16[512,1536]{1,0:T(8,128)(2,1)S(1)}, f32[8,128]{1,0:T(8,128)S(1)}) custom-call(s32[4]{0:T(128)S(1)} %pad_add_fusion.place, bf16[64,1536]{1,0:T(8,128)(2,1)S(1)} %copy-done.18, bf16[64,1536]{1,0:T(8,128)(2,1)} %collective-permute-done.3.refs_1_, bf16[64,1536]{1,0:T(8,128)(2,1)} %collective-permute-done.4.refs_2_, ...), custom_call_target="tpu_custom_call" | custom-call | flops 23253221376 | bytes 5505024 | tf_op jit(solution)/shard_map/pallas_call | solution.py:162
  57.2 1.4 convert_element_type.15
  58.7 6.4 %all-to-all-start.1 = ((f16[8,64,1792]{2,1,0:T(8,128)(2,1)}), f16[8,64,1792]{2,1,0:T(8,128)(2,1)}, u32[]{:S(2)}, u32[]{:S(2)}) async-start(f16[8,64,1792]{2,1,0:T(8,128)(2,1)} %bitcast.10), calls=%async_computation.1 | async-start | bytes 3670016 | tf_op jit(solution)/shard_map/all_to_all | solution.py:56
  65.2 3.0 %collective-permute-done.12.refs_3_ = bf16[64,3840]{1,0:T(8,128)(2,1)} collective-permute-done((bf16[64,3840]{1,0:T(8,128)(2,1)S(1)}, bf16[64,3840]{1,0:T(8,128)(2,1)}, u32[]{:S(2)}, u32[]{:S(2)}) %collective-permute-start.12) | collective-permute-done | bytes 491552 | tf_op jit(solution)/shard_map/ppermute | solution.py:48
  69.8 1.5 collective-permute-done.13.refs_4_
  73.0 1.8 copy-done.16
  74.8 7.3 %shard_map.165 = (f32[512,1408]{1,0:T(8,128)S(1)}, bf16[512,1536]{1,0:T(8,128)(2,1)S(1)}, bf16[1536,768]{1,0:T(8,128)(2,1)S(1)}) custom-call(s32[4]{0:T(128)S(1)} %pad_add_fusion.place, bf16[64,3840]{1,0:T(8,128)(2,1)S(1)} %copy-done.17, bf16[64,3840]{1,0:T(8,128)(2,1)} %collective-permute-done.10.refs_1_, bf16[64,3840]{1,0:T(8,128)(2,1)} %collective-permute-done.11.refs_2_, ...), custom_call_target="tpu_custom_call" | custom-call | flops 26776436736 | bytes 4325376 | tf_op jit(solution)/shard_map/pallas_call | solution.py:219
  82.0 1.4 copy-done.5
  87.0 5.6 %all-to-all-start.2 = ((f16[8,64,1408]{2,1,0:T(8,128)(2,1)}), f16[8,64,1408]{2,1,0:T(8,128)(2,1)S(1)}, u32[]{:S(2)}, u32[]{:S(2)}) async-start(f16[8,64,1408]{2,1,0:T(8,128)(2,1)} %bitcast.5), calls=%async_computation.2 | async-start | bytes 2883584 | tf_op jit(solution)/shard_map/all_to_all | solution.py:56
  92.6 3.6 %convert_element_type.17.first = f32[8,64,1792]{2,1,0:T(8,128)} convert(f16[8,64,1792]{2,1,0:T(8,128)(2,1)} %all-to-all-done.1) | non-fusion elementwise | flops 917504 | bytes 5505024 | tf_op jit(solution)/shard_map/convert_element_type | solution.py:520
  96.2 13.6 %all-to-all-done.2 = f16[8,64,1408]{2,1,0:T(8,128)(2,1)S(1)} async-done(((f16[8,64,1408]{2,1,0:T(8,128)(2,1)}), f16[8,64,1408]{2,1,0:T(8,128)(2,1)S(1)}, u32[]{:S(2)}, u32[]{:S(2)}) %all-to-all-start.2) | async-done | bytes 1441824 | tf_op jit(solution)/shard_map/all_to_all | solution.py:56
  110.0 1.8 copy-done
  111.9 3.1 %shard_map.166 = (bf16[8,64,1792]{2,1,0:T(8,128)(2,1)S(1)}, f32[64,384]{1,0:T(8,128)S(1)}, bf16[8,48,896]{2,1,0:T(8,128)(2,1)S(1)}) custom-call(f32[8,64,1792]{2,1,0:T(8,128)S(1)} %copy-done, f32[8,64,1408]{2,1,0:T(8,128)S(1)} %convert_element_type.18.second, f32[8,48,896]{2,1,0:T(8,128)} %all-to-all-done.b_parts), custom_call_target="tpu_custom_call" | custom-call | flops 176160768 | bytes 6553600 | tf_op jit(solution)/shard_map/pallas_call | solution.py:278
  117.1 5.6 %all-to-all-start.3 = ((bf16[8,64,1792]{2,1,0:T(8,128)(2,1)}), bf16[8,64,1792]{2,1,0:T(8,128)(2,1)S(1)}, u32[]{:S(2)}, u32[]{:S(2)}) async-start(bf16[8,64,1792]{2,1,0:T(8,128)(2,1)} %copy-done.7), calls=%async_computation.3 | async-start | bytes 3670016 | tf_op jit(solution)/shard_map/all_to_all | solution.py:56
  124.0 1.9 collective-permute-start.20
  125.9 1.7 collective-permute-start.19
  127.5 1.6 collective-permute-start.18
  129.1 1.4 copy-done.11
  130.5 4.3 %shard_map.168.selected = bf16[384,512]{1,0:T(8,128)(2,1)S(1)} custom-call(s32[4]{0:T(128)S(1)} %pad_add_fusion.place, bf16[512,1536]{1,0:T(8,128)(2,1)S(1)} %copy-done.9, bf16[512,1536]{1,0:T(8,128)(2,1)S(1)} %copy-done.11), custom_call_target="tpu_custom_call" | custom-call | flops 603979776 | bytes 3145728 | tf_op jit(solution)/shard_map/pallas_call | solution.py:369
  136.3 2.4 %shard_map.167 = bf16[8,112,896]{2,1,0:T(8,128)(2,1)} custom-call(bf16[8,48,896]{2,1,0:T(8,128)(2,1)} %copy-done.14, f32[64,384]{1,0:T(8,128)} %add_add_fusion.g), custom_call_target="tpu_custom_call" | custom-call | tf_op jit(solution)/shard_map/pallas_call | solution.py:347
  138.7 5.4 %all-to-all-done.3 = bf16[8,64,1792]{2,1,0:T(8,128)(2,1)S(1)} async-done(((bf16[8,64,1792]{2,1,0:T(8,128)(2,1)}), bf16[8,64,1792]{2,1,0:T(8,128)(2,1)S(1)}, u32[]{:S(2)}, u32[]{:S(2)}) %all-to-all-start.3) | async-done | bytes 1835040 | tf_op jit(solution)/shard_map/all_to_all | solution.py:56
  144.1 5.6 %all-to-all-start.4 = ((bf16[8,112,896]{2,1,0:T(8,128)(2,1)}), bf16[8,112,896]{2,1,0:T(8,128)(2,1)S(1)}, u32[]{:S(2)}, u32[]{:S(2)}) async-start(bf16[8,112,896]{2,1,0:T(8,128)(2,1)} %shard_map.167), calls=%async_computation.4 | async-start | bytes 3211264 | tf_op jit(solution)/shard_map/all_to_all | solution.py:56
  149.7 1.8 copy-done.2
  151.5 1.8 copy-done.4
  153.2 1.8 shard_map.170
  155.2 1.8 shard_map.171.refs_0_
  157.0 1.6 collective-permute-done.21.refs_1_
  160.5 2.3 %collective-permute-start.23 = (bf16[64,1536]{1,0:T(8,128)(2,1)S(1)}, bf16[64,1536]{1,0:T(8,128)(2,1)S(1)}, u32[]{:S(2)}, u32[]{:S(2)}) collective-permute-start(bf16[64,1536]{1,0:T(8,128)(2,1)S(1)} %get-tuple-element.74), channel_id=1, source_target_pairs={{0,6},{2,0},{4,2},{6,4},{1,7},{3,1},{5,3},{7,5},{8,14},{10,8},{12,... | collective-permute-start | bytes 589832 | tf_op jit(solution)/shard_map/ppermute | solution.py:52
  163.7 5.0 %all-to-all-done.4.merged = bf16[8,112,896]{2,1,0:T(8,128)(2,1)S(1)} async-done(((bf16[8,112,896]{2,1,0:T(8,128)(2,1)}), bf16[8,112,896]{2,1,0:T(8,128)(2,1)S(1)}, u32[]{:S(2)}, u32[]{:S(2)}) %all-to-all-start.4) | async-done | bytes 1605664 | tf_op jit(solution)/shard_map/all_to_all | solution.py:56
  168.7 1.7 copy-done.6
  170.3 1.5 shard_map.169
  173.8 5.6 %all-to-all-start.5 = ((bf16[4,16,2688]{2,1,0:T(8,128)(2,1)}), bf16[4,16,2688]{2,1,0:T(8,128)(2,1)S(1)}, u32[]{:S(2)}, u32[]{:S(2)}) async-start(bf16[4,16,2688]{2,1,0:T(8,128)(2,1)} %get-tuple-element.78), calls=%async_computation.5 | async-start | bytes 688128 | tf_op jit(solution)/shard_map/all_to_all | solution.py:56
  180.2 11.4 %all-to-all-done.5.others = bf16[4,16,2688]{2,1,0:T(8,128)(2,1)S(1)} async-done(((bf16[4,16,2688]{2,1,0:T(8,128)(2,1)}), bf16[4,16,2688]{2,1,0:T(8,128)(2,1)S(1)}, u32[]{:S(2)}, u32[]{:S(2)}) %all-to-all-start.5) | async-done | bytes 344096 | tf_op jit(solution)/shard_map/all_to_all | solution.py:56
  192.4 1.8 shard_map.174
  (84 shorter events, 24.9 us)
Async XLA Ops:
  2.2 16.7 %collective-permute-start.2 = (bf16[16,5376]{1,0:T(8,128)(2,1)}, bf16[16,5376]{1,0:T(8,128)(2,1)S(1)}, u32[]{:S(2)}, u32[]{:S(2)}) collective-permute-start(bf16[16,5376]{1,0:T(8,128)(2,1)} %shard_map.162.refs_0_), channel_id=1, source_target_pairs={{0,8},{8,16},{16,24},{24,0},{1,9},{9,17},{17,25},{25,1},{2,10},{10... | collective-permute-start | bytes 516104 | tf_op jit(solution)/shard_map/ppermute | solution.py:48
  5.4 14.7 %collective-permute-start.1 = (bf16[16,5376]{1,0:T(8,128)(2,1)}, bf16[16,5376]{1,0:T(8,128)(2,1)S(1)}, u32[]{:S(2)}, u32[]{:S(2)}) collective-permute-start(bf16[16,5376]{1,0:T(8,128)(2,1)} %shard_map.162.refs_0_), channel_id=1, source_target_pairs={{0,16},{8,24},{16,0},{24,8},{1,17},{9,25},{17,1},{25,9},{2,18},{10... | collective-permute-start | bytes 516104 | tf_op jit(solution)/shard_map/ppermute | solution.py:48
  9.9 12.6 %collective-permute-start = (bf16[16,5376]{1,0:T(8,128)(2,1)}, bf16[16,5376]{1,0:T(8,128)(2,1)S(1)}, u32[]{:S(2)}, u32[]{:S(2)}) collective-permute-start(bf16[16,5376]{1,0:T(8,128)(2,1)} %shard_map.162.refs_0_), channel_id=1, source_target_pairs={{0,24},{8,0},{16,8},{24,16},{1,25},{9,1},{17,9},{25,17},{2,26},{10... | collective-permute-start | bytes 516104 | tf_op jit(solution)/shard_map/ppermute | solution.py:48
  18.9 3.7 %copy-start.20 = (bf16[16,5376]{1,0:T(8,128)(2,1)}, bf16[16,5376]{1,0:T(8,128)(2,1)S(1)}, u32[]{:S(2)}) copy-start(bf16[16,5376]{1,0:T(8,128)(2,1)S(1)} %collective-permute-done.2.refs_3_) | copy-start | bytes 516100
  20.2 2.4 %copy-start.21 = (bf16[16,5376]{1,0:T(8,128)(2,1)}, bf16[16,5376]{1,0:T(8,128)(2,1)S(1)}, u32[]{:S(2)}) copy-start(bf16[16,5376]{1,0:T(8,128)(2,1)S(1)} %collective-permute-done.1.refs_2_) | copy-start | bytes 516100
  25.3 16.7 %collective-permute-start.5 = (bf16[64,1536]{1,0:T(8,128)(2,1)}, bf16[64,1536]{1,0:T(8,128)(2,1)}, u32[]{:S(2)}, u32[]{:S(2)}) collective-permute-start(bf16[64,1536]{1,0:T(8,128)(2,1)} %get-tuple-element.45.refs_0_), channel_id=1, source_target_pairs={{0,2},{2,4},{4,6},{6,0},{1,3},{3,5},{5,7},{7,1},{8,10},{10,12},{12... | collective-permute-start | bytes 589832 | tf_op jit(solution)/shard_map/ppermute | solution.py:48
  26.9 15.6 %collective-permute-start.4 = (bf16[64,1536]{1,0:T(8,128)(2,1)}, bf16[64,1536]{1,0:T(8,128)(2,1)}, u32[]{:S(2)}, u32[]{:S(2)}) collective-permute-start(bf16[64,1536]{1,0:T(8,128)(2,1)} %get-tuple-element.45.refs_0_), channel_id=1, source_target_pairs={{0,4},{2,6},{4,0},{6,2},{1,5},{3,7},{5,1},{7,3},{8,12},{10,14},{12... | collective-permute-start | bytes 589832 | tf_op jit(solution)/shard_map/ppermute | solution.py:48
  29.8 12.8 %collective-permute-start.3 = (bf16[64,1536]{1,0:T(8,128)(2,1)}, bf16[64,1536]{1,0:T(8,128)(2,1)}, u32[]{:S(2)}, u32[]{:S(2)}) collective-permute-start(bf16[64,1536]{1,0:T(8,128)(2,1)} %get-tuple-element.45.refs_0_), channel_id=1, source_target_pairs={{0,6},{2,0},{4,2},{6,4},{1,7},{3,1},{5,3},{7,5},{8,14},{10,8},{12,... | collective-permute-start | bytes 589832 | tf_op jit(solution)/shard_map/ppermute | solution.py:48
  32.0 10.0 %copy-start.18 = (bf16[64,1536]{1,0:T(8,128)(2,1)S(1)}, bf16[64,1536]{1,0:T(8,128)(2,1)}, u32[]{:S(2)}) copy-start(bf16[64,1536]{1,0:T(8,128)(2,1)} %get-tuple-element.45.refs_0_) | copy-start | bytes 589828
  32.0 11.1 %copy-start.17 = (bf16[64,3840]{1,0:T(8,128)(2,1)S(1)}, bf16[64,3840]{1,0:T(8,128)(2,1)}, u32[]{:S(2)}) copy-start(bf16[64,3840]{1,0:T(8,128)(2,1)} %get-tuple-element.52.refs_0_) | copy-start | bytes 1474564
  33.2 13.7 %copy-start.1 = (bf16[1536,896]{1,0:T(8,128)(2,1)S(1)}, bf16[1536,896]{1,0:T(8,128)(2,1)}, u32[]{:S(2)}) copy-start(bf16[1536,896]{1,0:T(8,128)(2,1)} %gate.3) | copy-start | bytes 8257540
  33.2 25.5 %all-to-all-start = ((f32[8,48,896]{2,1,0:T(8,128)}), f32[8,48,896]{2,1,0:T(8,128)}, u32[]{:S(2)}, u32[]{:S(2)}) async-start(f32[8,48,896]{2,1,0:T(8,128)} %broadcast_in_dim.2), calls=%async_computation | async-start | bytes 2752512 | tf_op jit(solution)/shard_map/all_to_all | solution.py:56
  42.0 1.8 collective-permute-start.6
  42.0 2.6 %collective-permute-start.9 = (bf16[64,1536]{1,0:T(8,128)(2,1)}, bf16[64,1536]{1,0:T(8,128)(2,1)}, u32[]{:S(2)}, u32[]{:S(2)}) collective-permute-start(bf16[64,1536]{1,0:T(8,128)(2,1)} %collective-permute-done.5.refs_3_), channel_id=1, source_target_pairs={{0,1},{1,0},{2,3},{3,2},{4,5},{5,4},{6,7},{7,6},{8,9},{9,8},{10,11... | collective-permute-start | bytes 589832 | tf_op jit(solution)/shard_map/ppermute | solution.py:48
  42.5 4.4 %collective-permute-start.8 = (bf16[64,1536]{1,0:T(8,128)(2,1)}, bf16[64,1536]{1,0:T(8,128)(2,1)}, u32[]{:S(2)}, u32[]{:S(2)}) collective-permute-start(bf16[64,1536]{1,0:T(8,128)(2,1)} %collective-permute-done.4.refs_2_), channel_id=1, source_target_pairs={{0,1},{1,0},{2,3},{3,2},{4,5},{5,4},{6,7},{7,6},{8,9},{9,8},{10,11... | collective-permute-start | bytes 589832 | tf_op jit(solution)/shard_map/ppermute | solution.py:48
  42.6 4.3 %collective-permute-start.7 = (bf16[64,1536]{1,0:T(8,128)(2,1)}, bf16[64,1536]{1,0:T(8,128)(2,1)}, u32[]{:S(2)}, u32[]{:S(2)}) collective-permute-start(bf16[64,1536]{1,0:T(8,128)(2,1)} %collective-permute-done.3.refs_1_), channel_id=1, source_target_pairs={{0,1},{1,0},{2,3},{3,2},{4,5},{5,4},{6,7},{7,6},{8,9},{9,8},{10,11... | collective-permute-start | bytes 589832 | tf_op jit(solution)/shard_map/ppermute | solution.py:48
  43.1 25.1 %collective-permute-start.12 = (bf16[64,3840]{1,0:T(8,128)(2,1)S(1)}, bf16[64,3840]{1,0:T(8,128)(2,1)}, u32[]{:S(2)}, u32[]{:S(2)}) collective-permute-start(bf16[64,3840]{1,0:T(8,128)(2,1)S(1)} %copy-done.17), channel_id=1, source_target_pairs={{0,2},{2,4},{4,6},{6,0},{1,3},{3,5},{5,7},{7,1},{8,10},{10,12},{12... | collective-permute-start | bytes 1474568 | tf_op jit(solution)/shard_map/ppermute | solution.py:48
  43.8 24.4 %collective-permute-start.11 = (bf16[64,3840]{1,0:T(8,128)(2,1)S(1)}, bf16[64,3840]{1,0:T(8,128)(2,1)}, u32[]{:S(2)}, u32[]{:S(2)}) collective-permute-start(bf16[64,3840]{1,0:T(8,128)(2,1)S(1)} %copy-done.17), channel_id=1, source_target_pairs={{0,4},{2,6},{4,0},{6,2},{1,5},{3,7},{5,1},{7,3},{8,12},{10,14},{12... | collective-permute-start | bytes 1474568 | tf_op jit(solution)/shard_map/ppermute | solution.py:48
  44.6 24.2 %collective-permute-start.10 = (bf16[64,3840]{1,0:T(8,128)(2,1)S(1)}, bf16[64,3840]{1,0:T(8,128)(2,1)}, u32[]{:S(2)}, u32[]{:S(2)}) collective-permute-start(bf16[64,3840]{1,0:T(8,128)(2,1)S(1)} %copy-done.17), channel_id=1, source_target_pairs={{0,6},{2,0},{4,2},{6,4},{1,7},{3,1},{5,3},{7,5},{8,14},{10,8},{12,... | collective-permute-start | bytes 1474568 | tf_op jit(solution)/shard_map/ppermute | solution.py:48
  46.9 1.8 copy-start.3
  58.7 14.3 %copy-start.9 = (bf16[512,1536]{1,0:T(8,128)(2,1)S(1)}, bf16[512,1536]{1,0:T(8,128)(2,1)}, u32[]{:S(2)}) copy-start(bf16[512,1536]{1,0:T(8,128)(2,1)} %copy-done.8) | copy-start | bytes 4718596
  58.7 28.3 %all-to-all-start.1 = ((f16[8,64,1792]{2,1,0:T(8,128)(2,1)}), f16[8,64,1792]{2,1,0:T(8,128)(2,1)}, u32[]{:S(2)}, u32[]{:S(2)}) async-start(f16[8,64,1792]{2,1,0:T(8,128)(2,1)} %bitcast.10), calls=%async_computation.1 | async-start | bytes 3670016 | tf_op jit(solution)/shard_map/all_to_all | solution.py:56
  68.8 2.5 %collective-permute-start.13 = (bf16[64,3840]{1,0:T(8,128)(2,1)S(1)}, bf16[64,3840]{1,0:T(8,128)(2,1)S(1)}, u32[]{:S(2)}, u32[]{:S(2)}) collective-permute-start(bf16[64,3840]{1,0:T(8,128)(2,1)S(1)} %copy-done.17), channel_id=1, source_target_pairs={{0,1},{1,0},{2,3},{3,2},{4,5},{5,4},{6,7},{7,6},{8,9},{9,8},{10,11... | collective-permute-start | bytes 1474568 | tf_op jit(solution)/shard_map/ppermute | solution.py:48
  68.8 2.8 %collective-permute-start.14 = (bf16[64,3840]{1,0:T(8,128)(2,1)}, bf16[64,3840]{1,0:T(8,128)(2,1)S(1)}, u32[]{:S(2)}, u32[]{:S(2)}) collective-permute-start(bf16[64,3840]{1,0:T(8,128)(2,1)} %collective-permute-done.10.refs_1_), channel_id=1, source_target_pairs={{0,1},{1,0},{2,3},{3,2},{4,5},{5,4},{6,7},{7,6},{8,9},{9,8},{10,11... | collective-permute-start | bytes 1474568 | tf_op jit(solution)/shard_map/ppermute | solution.py:48
  69.3 3.0 %collective-permute-start.15 = (bf16[64,3840]{1,0:T(8,128)(2,1)}, bf16[64,3840]{1,0:T(8,128)(2,1)S(1)}, u32[]{:S(2)}, u32[]{:S(2)}) collective-permute-start(bf16[64,3840]{1,0:T(8,128)(2,1)} %collective-permute-done.11.refs_2_), channel_id=1, source_target_pairs={{0,1},{1,0},{2,3},{3,2},{4,5},{5,4},{6,7},{7,6},{8,9},{9,8},{10,11... | collective-permute-start | bytes 1474568 | tf_op jit(solution)/shard_map/ppermute | solution.py:48
  69.3 3.7 %collective-permute-start.16 = (bf16[64,3840]{1,0:T(8,128)(2,1)}, bf16[64,3840]{1,0:T(8,128)(2,1)S(1)}, u32[]{:S(2)}, u32[]{:S(2)}) collective-permute-start(bf16[64,3840]{1,0:T(8,128)(2,1)} %collective-permute-done.12.refs_3_), channel_id=1, source_target_pairs={{0,1},{1,0},{2,3},{3,2},{4,5},{5,4},{6,7},{7,6},{8,9},{9,8},{10,11... | collective-permute-start | bytes 1474568 | tf_op jit(solution)/shard_map/ppermute | solution.py:48
  73.0 1.8 copy-start.16
  82.0 1.4 copy-start.5
  87.0 22.8 %all-to-all-start.2 = ((f16[8,64,1408]{2,1,0:T(8,128)(2,1)}), f16[8,64,1408]{2,1,0:T(8,128)(2,1)S(1)}, u32[]{:S(2)}, u32[]{:S(2)}) async-start(f16[8,64,1408]{2,1,0:T(8,128)(2,1)} %bitcast.5), calls=%async_computation.2 | async-start | bytes 2883584 | tf_op jit(solution)/shard_map/all_to_all | solution.py:56
  109.8 2.0 %copy-start = (f32[8,64,1792]{2,1,0:T(8,128)S(1)}, f32[8,64,1792]{2,1,0:T(8,128)}, u32[]{:S(2)}) copy-start(f32[8,64,1792]{2,1,0:T(8,128)} %convert_element_type.17.first) | copy-start | bytes 11010052
  115.0 1.3 copy-start.7
  117.1 27.0 %all-to-all-start.3 = ((bf16[8,64,1792]{2,1,0:T(8,128)(2,1)}), bf16[8,64,1792]{2,1,0:T(8,128)(2,1)S(1)}, u32[]{:S(2)}, u32[]{:S(2)}) async-start(bf16[8,64,1792]{2,1,0:T(8,128)(2,1)} %copy-done.7), calls=%async_computation.3 | async-start | bytes 3670016 | tf_op jit(solution)/shard_map/all_to_all | solution.py:56
  122.6 1.3 collective-permute-start.17
  124.0 11.7 %collective-permute-start.20 = (f32[64,384]{1,0:T(8,128)S(1)}, f32[64,384]{1,0:T(8,128)S(1)}, u32[]{:S(2)}, u32[]{:S(2)}) collective-permute-start(f32[64,384]{1,0:T(8,128)S(1)} %add.23), channel_id=1, source_target_pairs={{0,4},{2,6},{4,0},{6,2},{1,5},{3,7},{5,1},{7,3},{8,12},{10,14},{12... | collective-permute-start | bytes 294920 | tf_op jit(solution)/shard_map/ppermute | solution.py:48
  125.9 9.7 %collective-permute-start.19 = (f32[64,384]{1,0:T(8,128)S(1)}, f32[64,384]{1,0:T(8,128)S(1)}, u32[]{:S(2)}, u32[]{:S(2)}) collective-permute-start(f32[64,384]{1,0:T(8,128)S(1)} %add.23), channel_id=1, source_target_pairs={{0,2},{2,4},{4,6},{6,0},{1,3},{3,5},{5,7},{7,1},{8,10},{10,12},{12... | collective-permute-start | bytes 294920 | tf_op jit(solution)/shard_map/ppermute | solution.py:48
  127.5 8.1 %collective-permute-start.18 = (f32[64,384]{1,0:T(8,128)S(1)}, f32[64,384]{1,0:T(8,128)S(1)}, u32[]{:S(2)}, u32[]{:S(2)}) collective-permute-start(f32[64,384]{1,0:T(8,128)S(1)} %add.23), channel_id=1, source_target_pairs={{0,6},{2,0},{4,2},{6,4},{1,7},{3,1},{5,3},{7,5},{8,14},{10,8},{12,... | collective-permute-start | bytes 294920 | tf_op jit(solution)/shard_map/ppermute | solution.py:48
  129.1 1.4 copy-start.11
  144.1 24.6 %all-to-all-start.4 = ((bf16[8,112,896]{2,1,0:T(8,128)(2,1)}), bf16[8,112,896]{2,1,0:T(8,128)(2,1)S(1)}, u32[]{:S(2)}, u32[]{:S(2)}) async-start(bf16[8,112,896]{2,1,0:T(8,128)(2,1)} %shard_map.167), calls=%async_computation.4 | async-start | bytes 3211264 | tf_op jit(solution)/shard_map/all_to_all | solution.py:56
  149.7 1.8 copy-start.2
  151.5 1.8 copy-start.4
  155.1 3.5 %collective-permute-start.21 = (f32[256,1536]{1,0:T(8,128)S(1)}, f32[256,1536]{1,0:T(8,128)S(1)}, u32[]{:S(2)}, u32[]{:S(2)}) collective-permute-start(f32[256,1536]{1,0:T(8,128)S(1)} %shard_map.170), channel_id=1, source_target_pairs={{0,1},{1,0},{2,3},{3,2},{4,5},{5,4},{6,7},{7,6},{8,9},{9,8},{10,11... | collective-permute-start | bytes 4718600 | tf_op jit(solution)/shard_map/ppermute | solution.py:48
  157.0 11.7 %copy-start.13 = (bf16[384,512]{1,0:T(8,128)(2,1)S(1)}, bf16[384,512]{1,0:T(8,128)(2,1)}, u32[]{:S(2)}) copy-start(bf16[384,512]{1,0:T(8,128)(2,1)} %copy-done.12) | copy-start | bytes 1179652
  159.5 12.4 %collective-permute-start.22 = (bf16[64,1536]{1,0:T(8,128)(2,1)}, bf16[64,1536]{1,0:T(8,128)(2,1)S(1)}, u32[]{:S(2)}, u32[]{:S(2)}) collective-permute-start(bf16[64,1536]{1,0:T(8,128)(2,1)} %get-tuple-element.73), channel_id=1, source_target_pairs={{0,2},{2,4},{4,6},{6,0},{1,3},{3,5},{5,7},{7,1},{8,10},{10,12},{12... | collective-permute-start | bytes 589832 | tf_op jit(solution)/shard_map/ppermute | solution.py:52
  160.5 11.4 %collective-permute-start.23 = (bf16[64,1536]{1,0:T(8,128)(2,1)S(1)}, bf16[64,1536]{1,0:T(8,128)(2,1)S(1)}, u32[]{:S(2)}, u32[]{:S(2)}) collective-permute-start(bf16[64,1536]{1,0:T(8,128)(2,1)S(1)} %get-tuple-element.74), channel_id=1, source_target_pairs={{0,6},{2,0},{4,2},{6,4},{1,7},{3,1},{5,3},{7,5},{8,14},{10,8},{12,... | collective-permute-start | bytes 589832 | tf_op jit(solution)/shard_map/ppermute | solution.py:52
  162.7 10.3 %collective-permute-start.24 = (bf16[64,1536]{1,0:T(8,128)(2,1)S(1)}, bf16[64,1536]{1,0:T(8,128)(2,1)S(1)}, u32[]{:S(2)}, u32[]{:S(2)}) collective-permute-start(bf16[64,1536]{1,0:T(8,128)(2,1)S(1)} %get-tuple-element.75), channel_id=1, source_target_pairs={{0,4},{2,6},{4,0},{6,2},{1,5},{3,7},{5,1},{7,3},{8,12},{10,14},{12... | collective-permute-start | bytes 589832 | tf_op jit(solution)/shard_map/ppermute | solution.py:52
  168.7 1.7 copy-start.6
  173.8 17.8 %copy-start.15 = (f32[16,2688]{1,0:T(8,128)}, f32[16,2688]{1,0:T(8,128)S(1)}, u32[]{:S(2)}) copy-start(f32[16,2688]{1,0:T(8,128)S(1)} %get-tuple-element.77.kept) | copy-start | bytes 516100
  173.8 17.8 %all-to-all-start.5 = ((bf16[4,16,2688]{2,1,0:T(8,128)(2,1)}), bf16[4,16,2688]{2,1,0:T(8,128)(2,1)S(1)}, u32[]{:S(2)}, u32[]{:S(2)}) async-start(bf16[4,16,2688]{2,1,0:T(8,128)(2,1)} %get-tuple-element.78), calls=%async_computation.5 | async-start | bytes 688128 | tf_op jit(solution)/shard_map/all_to_all | solution.py:56
  (6 other events, 5.3 us)

commit v3 on v2

--- a/solution.py
+++ b/solution.py
@@ -105,6 +105,24 @@
         in_specs=[SMEM] + [VMEM] * len(parts),
         out_specs=(VMEM, VMEM),
     )(here, *parts)
+
+
+def order_factors(b_parts):
+    share, units = b_parts.shape[1] // 3, b_parts.shape[2]
+
+    def kernel(b_parts, b):
+        for i in range(3):
+            for r in range(NROW):
+                b[i, r * share : (r + 1) * share, :] = b_parts[r, i * share : (i + 1) * share, :]
+
+    return pl.pallas_call(
+        kernel,
+        out_shape=shape((3, NROW * share, units), F32),
+        in_specs=[VMEM],
+        out_specs=VMEM,
+        compiler_params=PARAMS,
+        cost_estimate=cost(0, b_parts, b_parts),
+    )(b_parts)
 
 
 def panel_moves(place, pieces, first, size, target, sems):
@@ -235,18 +253,15 @@
     )(place, *pieces, x, down_w, exponents)
 
 
-def swiglu_back(first, second, b_parts):
+def swiglu_back(first, second, b):
     per, lanes = second.shape[1:]
-    share, units = b_parts.shape[1] // 3, b_parts.shape[2]
-    rank = share * NROW
+    rank, units = b.shape[1:]
+    share = rank // NROW
     ranks = 3 * rank
     sizes = [units] * 3 + [rank] * 3
     starts = [0, units, 0, units, units + rank, units + 2 * rank]
 
-    def kernel(first, second, b_parts, wide, g_out, factor_out, b):
-        for i in range(3):
-            for r in range(NROW):
-                b[i, r * share : (r + 1) * share, :] = b_parts[r, i * share : (i + 1) * share, :]
+    def kernel(first, second, b, wide, g_out, factor_out):
         scales = [jnp.exp2(second[r, 0:1, lanes - 128 :]) for r in range(NROW)]
 
         def total(i):
@@ -284,10 +299,9 @@
         ),
         in_specs=[VMEM] * 3,
         out_specs=(VMEM,) * 3,
-        scratch_shapes=[pltpu.VMEM((3, rank, units), F32)],
         compiler_params=PARAMS,
         cost_estimate=cost(24 * per * rank * units, first, second),
-    )(first, second, b_parts)
+    )(first, second, b)
 
 
 def backward(which, d_all, gate_w, up_w):
@@ -515,10 +529,10 @@
         place, with_core(late_pieces), x, down_w, exponents, ranks, own_features
     )
     sums_x, part_dy = lax.optimization_barrier((exchange(part_x, ROW), half(part_dy)))
-    selected = select(place, x, dy, own_features)
-    wide, g, factor_parts = swiglu_back(
-        sums_x.astype(F32), exchange(part_dy, ROW).astype(F32), b_parts
+    sums_dy, selected, b = lax.optimization_barrier(
+        (exchange(part_dy, ROW), select(place, x, dy, own_features), order_factors(b_parts))
     )
+    wide, g, factor_parts = swiglu_back(sums_x.astype(F32), sums_dy.astype(F32), b)
 
     d_all = exchange(wide, ROW).reshape(rows, 2 * units)
 

time: 196 us -> 196 us (level)
  waiting for transfers between devices: 57.4 us -> 66.4 us
  starting transfers between devices: 69.1 us -> 61.3 us
  local copies, waits for them, and re-layouts: 21.9 us -> 19.3 us
    ppermute x22, waiting for transfers between devices: 19.7 us -> 32.1 us  [from_next(): return lax.ppermute(a, axis, [(j, (j - s) % n) for j in range(n)])]
    ppermute x22, starting transfers between devices: 27.3 us -> 22.1 us  [from_next(): return lax.ppermute(a, axis, [(j, (j - s) % n) for j in range(n)])]
    unnamed x46 -> x44, local copies, waits for them, and re-layouts: 20 us -> 17.4 us
    all_to_all x6, waiting for transfers between devices: 36.6 us -> 34.1 us  [exchange(): return lax.all_to_all(wide, axis, split_axis=0, concat_axis=0)]
  transfers between devices with their start and end apart: 31 -> 31, of which waited for: 18 -> 18; matrix products, arithmetic and copies ran while one was open for 5% -> 5% of each run, Pallas kernels for 14% -> 15%
where the time goes in v3:
time: 196 us; the launch traced here: 195 us
  waiting for transfers between devices  66.4 us (34%)
  starting transfers between devices  61.3 us (31%)
  Pallas kernels  36.9 us (19%)
  local copies, waits for them, and re-layouts  19.3 us (10%)
  other arithmetic  9.75 us (5%)
    all_to_all x6, starting transfers between devices, exchange(): return lax.all_to_all(wide, axis, split_axis=0, concat_axis=0)  36 us
    all_to_all x6, waiting for transfers between devices, exchange(): return lax.all_to_all(wide, axis, split_axis=0, concat_axis=0)  34.1 us
    ppermute x22, waiting for transfers between devices, from_next(): return lax.ppermute(a, axis, [(j, (j - s) % n) for j in range(n)])  32.1 us
    ppermute x22, starting transfers between devices, from_next(): return lax.ppermute(a, axis, [(j, (j - s) % n) for j in range(n)])  22.1 us
    unnamed x44, local copies, waits for them, and re-layouts  17.4 us
    pallas_call x1, Pallas kernels, forward_x(): pl.pallas_call(kernel, out_shape=(shape((rows, 2 * units), F32), shape((r...  7.36 us
    pallas_call x1, Pallas kernels, forward_dy(): pl.pallas_call(kernel, out_shape=(shape((rows, units + ranks + 128), F32)...  7.26 us
    pallas_call x1, Pallas kernels, select(): pl.pallas_call(kernel, out_shape=shape((2 * NZH * own_features, rows), BF...  4.33 us
  transfers between devices with their start and end apart: 31, of which 18 were waited for; matrix products, arithmetic and copies ran while one was open for 5% of the time, Pallas kernels for 15%

profile of v3, /device:TPU:34, one launch (start us, length us, event | category | flops | bytes accessed | tf_op | source)
XLA Modules:
  0.0 194.6 jit_solution(6633029207871506357)
XLA Ops:
  0.6 1.5 shard_map.162.refs_0_
  2.2 5.4 %collective-permute-start = (bf16[16,5376]{1,0:T(8,128)(2,1)}, bf16[16,5376]{1,0:T(8,128)(2,1)S(1)}, u32[]{:S(2)}, u32[]{:S(2)}) collective-permute-start(bf16[16,5376]{1,0:T(8,128)(2,1)} %shard_map.162.refs_0_), channel_id=1, source_target_pairs={{0,24},{8,0},{16,8},{24,16},{1,25},{9,1},{17,9},{25,17},{2,26},{10... | collective-permute-start | bytes 516104 | tf_op jit(solution)/shard_map/ppermute | solution.py:48
  7.6 1.4 collective-permute-start.1
  9.0 2.4 %collective-permute-start.2 = (bf16[16,5376]{1,0:T(8,128)(2,1)}, bf16[16,5376]{1,0:T(8,128)(2,1)S(1)}, u32[]{:S(2)}, u32[]{:S(2)}) collective-permute-start(bf16[16,5376]{1,0:T(8,128)(2,1)} %shard_map.162.refs_0_), channel_id=1, source_target_pairs={{0,8},{8,16},{16,24},{24,0},{1,9},{9,17},{17,25},{25,1},{2,10},{10... | collective-permute-start | bytes 516104 | tf_op jit(solution)/shard_map/ppermute | solution.py:48
  11.4 5.3 %collective-permute-done.refs_1_ = bf16[16,5376]{1,0:T(8,128)(2,1)S(1)} collective-permute-done((bf16[16,5376]{1,0:T(8,128)(2,1)}, bf16[16,5376]{1,0:T(8,128)(2,1)S(1)}, u32[]{:S(2)}, u32[]{:S(2)}) %collective-permute-start) | collective-permute-done | bytes 172064 | tf_op jit(solution)/shard_map/ppermute | solution.py:48
  16.6 7.8 %collective-permute-done.1.refs_2_ = bf16[16,5376]{1,0:T(8,128)(2,1)S(1)} collective-permute-done((bf16[16,5376]{1,0:T(8,128)(2,1)}, bf16[16,5376]{1,0:T(8,128)(2,1)S(1)}, u32[]{:S(2)}, u32[]{:S(2)}) %collective-permute-start.1) | collective-permute-done | bytes 172064 | tf_op jit(solution)/shard_map/ppermute | solution.py:48
  25.6 2.1 %shard_map.163 = (bf16[64,1536]{1,0:T(8,128)(2,1)}, bf16[64,3840]{1,0:T(8,128)(2,1)}) custom-call(s32[1]{0:T(128)} %bitcast.here, bf16[16,5376]{1,0:T(8,128)(2,1)} %shard_map.162.refs_0_, bf16[16,5376]{1,0:T(8,128)(2,1)} %copy-done.19, bf16[16,5376]{1,0:T(8,128)(2,1)} %copy-done.20, bf16[16,5376]{1,0:T(8,128)(2,1)} %copy-done.21), custom_call_target="tpu_custom_call" | custom-call | tf_op jit(solution)/shard_map/pallas_call | solution.py:99
  27.6 3.0 %collective-permute-start.3 = (bf16[64,1536]{1,0:T(8,128)(2,1)}, bf16[64,1536]{1,0:T(8,128)(2,1)}, u32[]{:S(2)}, u32[]{:S(2)}) collective-permute-start(bf16[64,1536]{1,0:T(8,128)(2,1)} %get-tuple-element.48.refs_0_), channel_id=1, source_target_pairs={{0,6},{2,0},{4,2},{6,4},{1,7},{3,1},{5,3},{7,5},{8,14},{10,8},{12,... | collective-permute-start | bytes 589832 | tf_op jit(solution)/shard_map/ppermute | solution.py:48
  34.4 6.0 %all-to-all-start = ((f32[8,48,896]{2,1,0:T(8,128)}), f32[8,48,896]{2,1,0:T(8,128)}, u32[]{:S(2)}, u32[]{:S(2)}) async-start(f32[8,48,896]{2,1,0:T(8,128)} %broadcast_in_dim.2), calls=%async_computation | async-start | bytes 2752512 | tf_op jit(solution)/shard_map/all_to_all | solution.py:56
  41.0 1.8 collective-permute-done.5.refs_3_
  43.8 1.7 collective-permute-start.11
  45.5 1.8 copy-done.3
  47.3 7.4 %shard_map.164 = (f32[512,1792]{1,0:T(8,128)S(1)}, bf16[512,1536]{1,0:T(8,128)(2,1)S(1)}, f32[8,128]{1,0:T(8,128)S(1)}) custom-call(s32[4]{0:T(128)S(1)} %pad_add_fusion.place, bf16[64,1536]{1,0:T(8,128)(2,1)S(1)} %copy-done.17, bf16[64,1536]{1,0:T(8,128)(2,1)} %collective-permute-done.3.refs_1_, bf16[64,1536]{1,0:T(8,128)(2,1)} %collective-permute-done.4.refs_2_, ...), custom_call_target="tpu_custom_call" | custom-call | flops 23253221376 | bytes 5505024 | tf_op jit(solution)/shard_map/pallas_call | solution.py:180
  55.8 1.4 convert_element_type.15
  57.3 5.8 %all-to-all-start.1 = ((f16[8,64,1792]{2,1,0:T(8,128)(2,1)}), f16[8,64,1792]{2,1,0:T(8,128)(2,1)}, u32[]{:S(2)}, u32[]{:S(2)}) async-start(f16[8,64,1792]{2,1,0:T(8,128)(2,1)} %bitcast.10), calls=%async_computation.1 | async-start | bytes 3670016 | tf_op jit(solution)/shard_map/all_to_all | solution.py:56
  63.1 5.9 %collective-permute-done.12.refs_3_ = bf16[64,3840]{1,0:T(8,128)(2,1)} collective-permute-done((bf16[64,3840]{1,0:T(8,128)(2,1)S(1)}, bf16[64,3840]{1,0:T(8,128)(2,1)}, u32[]{:S(2)}, u32[]{:S(2)}) %collective-permute-start.12) | collective-permute-done | bytes 491552 | tf_op jit(solution)/shard_map/ppermute | solution.py:48
  70.0 1.4 collective-permute-done.13.refs_4_
  73.2 1.8 copy-done.14
  76.0 7.3 %shard_map.165 = (f32[512,1408]{1,0:T(8,128)S(1)}, bf16[512,1536]{1,0:T(8,128)(2,1)S(1)}, bf16[1536,768]{1,0:T(8,128)(2,1)S(1)}) custom-call(s32[4]{0:T(128)S(1)} %pad_add_fusion.place, bf16[64,3840]{1,0:T(8,128)(2,1)S(1)} %copy-done.16, bf16[64,3840]{1,0:T(8,128)(2,1)} %collective-permute-done.10.refs_1_, bf16[64,3840]{1,0:T(8,128)(2,1)} %collective-permute-done.11.refs_2_, ...), custom_call_target="tpu_custom_call" | custom-call | flops 26776436736 | bytes 4325376 | tf_op jit(solution)/shard_map/pallas_call | solution.py:237
  83.3 1.4 copy-done.5
  84.7 1.3 convert_element_type.16
  86.0 5.7 %all-to-all-start.2 = ((f16[8,64,1408]{2,1,0:T(8,128)(2,1)}), f16[8,64,1408]{2,1,0:T(8,128)(2,1)}, u32[]{:S(2)}, u32[]{:S(2)}) async-start(f16[8,64,1408]{2,1,0:T(8,128)(2,1)} %bitcast.11), calls=%async_computation.2 | async-start | bytes 2883584 | tf_op jit(solution)/shard_map/all_to_all | solution.py:56
  91.7 4.3 %shard_map.166.selected = bf16[384,512]{1,0:T(8,128)(2,1)S(1)} custom-call(s32[4]{0:T(128)S(1)} %pad_add_fusion.place, bf16[512,1536]{1,0:T(8,128)(2,1)S(1)} %copy-done.9, bf16[512,1536]{1,0:T(8,128)(2,1)S(1)} %get-tuple-element.64.dy), custom_call_target="tpu_custom_call" | custom-call | flops 603979776 | bytes 3145728 | tf_op jit(solution)/shard_map/pallas_call | solution.py:383
  96.8 1.4 shard_map.167.b
  98.3 3.6 %convert_element_type.17.first = f32[8,64,1792]{2,1,0:T(8,128)} convert(f16[8,64,1792]{2,1,0:T(8,128)(2,1)} %all-to-all-done.1) | non-fusion elementwise | flops 917504 | bytes 5505024 | tf_op jit(solution)/shard_map/convert_element_type | solution.py:535
  101.9 8.1 %all-to-all-done.2 = f16[8,64,1408]{2,1,0:T(8,128)(2,1)} async-done(((f16[8,64,1408]{2,1,0:T(8,128)(2,1)}), f16[8,64,1408]{2,1,0:T(8,128)(2,1)}, u32[]{:S(2)}, u32[]{:S(2)}) %all-to-all-start.2) | async-done | bytes 1441824 | tf_op jit(solution)/shard_map/all_to_all | solution.py:56
  110.0 1.7 convert_element_type.18.second
  112.4 1.9 shard_map.168
  116.4 5.6 %all-to-all-start.3 = ((bf16[8,64,1792]{2,1,0:T(8,128)(2,1)}), bf16[8,64,1792]{2,1,0:T(8,128)(2,1)S(1)}, u32[]{:S(2)}, u32[]{:S(2)}) async-start(bf16[8,64,1792]{2,1,0:T(8,128)(2,1)} %copy-done.7), calls=%async_computation.3 | async-start | bytes 3670016 | tf_op jit(solution)/shard_map/all_to_all | solution.py:56
  122.0 1.3 collective-permute-done.17
  123.3 1.9 collective-permute-start.20
  127.3 3.2 %collective-permute-done.20 = f32[64,384]{1,0:T(8,128)S(1)} collective-permute-done((f32[64,384]{1,0:T(8,128)S(1)}, f32[64,384]{1,0:T(8,128)S(1)}, u32[]{:S(2)}, u32[]{:S(2)}) %collective-permute-start.20) | collective-permute-done | bytes 98336 | tf_op jit(solution)/shard_map/ppermute | solution.py:48
  130.5 1.6 collective-permute-done.19
  132.8 2.4 %shard_map.169 = bf16[8,112,896]{2,1,0:T(8,128)(2,1)} custom-call(bf16[8,48,896]{2,1,0:T(8,128)(2,1)} %copy-done.12, f32[64,384]{1,0:T(8,128)} %add_add_fusion.g), custom_call_target="tpu_custom_call" | custom-call | tf_op jit(solution)/shard_map/pallas_call | solution.py:361
  135.2 8.4 %all-to-all-done.3 = bf16[8,64,1792]{2,1,0:T(8,128)(2,1)S(1)} async-done(((bf16[8,64,1792]{2,1,0:T(8,128)(2,1)}), bf16[8,64,1792]{2,1,0:T(8,128)(2,1)S(1)}, u32[]{:S(2)}, u32[]{:S(2)}) %all-to-all-start.3) | async-done | bytes 1835040 | tf_op jit(solution)/shard_map/all_to_all | solution.py:56
  143.5 5.6 %all-to-all-start.4 = ((bf16[8,112,896]{2,1,0:T(8,128)(2,1)}), bf16[8,112,896]{2,1,0:T(8,128)(2,1)S(1)}, u32[]{:S(2)}, u32[]{:S(2)}) async-start(bf16[8,112,896]{2,1,0:T(8,128)(2,1)} %shard_map.169), calls=%async_computation.4 | async-start | bytes 3211264 | tf_op jit(solution)/shard_map/all_to_all | solution.py:56
  149.1 1.8 copy-done.2
  150.9 1.8 copy-done.4
  152.7 1.8 shard_map.171
  154.6 1.8 shard_map.172.refs_0_
  156.5 1.6 collective-permute-done.21.refs_1_
  159.0 3.2 %collective-permute-start.23 = (bf16[64,1536]{1,0:T(8,128)(2,1)S(1)}, bf16[64,1536]{1,0:T(8,128)(2,1)S(1)}, u32[]{:S(2)}, u32[]{:S(2)}) collective-permute-start(bf16[64,1536]{1,0:T(8,128)(2,1)S(1)} %get-tuple-element.80), channel_id=1, source_target_pairs={{0,6},{2,0},{4,2},{6,4},{1,7},{3,1},{5,3},{7,5},{8,14},{10,8},{12,... | collective-permute-start | bytes 589832 | tf_op jit(solution)/shard_map/ppermute | solution.py:52
  162.2 5.9 %all-to-all-done.4.merged = bf16[8,112,896]{2,1,0:T(8,128)(2,1)S(1)} async-done(((bf16[8,112,896]{2,1,0:T(8,128)(2,1)}), bf16[8,112,896]{2,1,0:T(8,128)(2,1)S(1)}, u32[]{:S(2)}, u32[]{:S(2)}) %all-to-all-start.4) | async-done | bytes 1605664 | tf_op jit(solution)/shard_map/all_to_all | solution.py:56
  168.1 1.7 copy-done.6
  169.8 1.5 shard_map.170
  172.4 7.2 %all-to-all-start.5 = ((bf16[4,16,2688]{2,1,0:T(8,128)(2,1)}), bf16[4,16,2688]{2,1,0:T(8,128)(2,1)S(1)}, u32[]{:S(2)}, u32[]{:S(2)}) async-start(bf16[4,16,2688]{2,1,0:T(8,128)(2,1)} %get-tuple-element.84), calls=%async_computation.5 | async-start | bytes 688128 | tf_op jit(solution)/shard_map/all_to_all | solution.py:56
  180.3 11.7 %all-to-all-done.5.others = bf16[4,16,2688]{2,1,0:T(8,128)(2,1)S(1)} async-done(((bf16[4,16,2688]{2,1,0:T(8,128)(2,1)}), bf16[4,16,2688]{2,1,0:T(8,128)(2,1)S(1)}, u32[]{:S(2)}, u32[]{:S(2)}) %all-to-all-start.5) | async-done | bytes 344096 | tf_op jit(solution)/shard_map/all_to_all | solution.py:56
  192.8 1.8 shard_map.175
  (83 shorter events, 21.4 us)
Async XLA Ops:
  2.2 14.5 %collective-permute-start = (bf16[16,5376]{1,0:T(8,128)(2,1)}, bf16[16,5376]{1,0:T(8,128)(2,1)S(1)}, u32[]{:S(2)}, u32[]{:S(2)}) collective-permute-start(bf16[16,5376]{1,0:T(8,128)(2,1)} %shard_map.162.refs_0_), channel_id=1, source_target_pairs={{0,24},{8,0},{16,8},{24,16},{1,25},{9,1},{17,9},{25,17},{2,26},{10... | collective-permute-start | bytes 516104 | tf_op jit(solution)/shard_map/ppermute | solution.py:48
  7.6 16.8 %collective-permute-start.1 = (bf16[16,5376]{1,0:T(8,128)(2,1)}, bf16[16,5376]{1,0:T(8,128)(2,1)S(1)}, u32[]{:S(2)}, u32[]{:S(2)}) collective-permute-start(bf16[16,5376]{1,0:T(8,128)(2,1)} %shard_map.162.refs_0_), channel_id=1, source_target_pairs={{0,16},{8,24},{16,0},{24,8},{1,17},{9,25},{17,1},{25,9},{2,18},{10... | collective-permute-start | bytes 516104 | tf_op jit(solution)/shard_map/ppermute | solution.py:48
  9.0 15.9 %collective-permute-start.2 = (bf16[16,5376]{1,0:T(8,128)(2,1)}, bf16[16,5376]{1,0:T(8,128)(2,1)S(1)}, u32[]{:S(2)}, u32[]{:S(2)}) collective-permute-start(bf16[16,5376]{1,0:T(8,128)(2,1)} %shard_map.162.refs_0_), channel_id=1, source_target_pairs={{0,8},{8,16},{16,24},{24,0},{1,9},{9,17},{17,25},{25,1},{2,10},{10... | collective-permute-start | bytes 516104 | tf_op jit(solution)/shard_map/ppermute | solution.py:48
  16.6 8.3 %copy-start.19 = (bf16[16,5376]{1,0:T(8,128)(2,1)}, bf16[16,5376]{1,0:T(8,128)(2,1)S(1)}, u32[]{:S(2)}) copy-start(bf16[16,5376]{1,0:T(8,128)(2,1)S(1)} %collective-permute-done.refs_1_) | copy-start | bytes 516100
  27.6 12.7 %collective-permute-start.3 = (bf16[64,1536]{1,0:T(8,128)(2,1)}, bf16[64,1536]{1,0:T(8,128)(2,1)}, u32[]{:S(2)}, u32[]{:S(2)}) collective-permute-start(bf16[64,1536]{1,0:T(8,128)(2,1)} %get-tuple-element.48.refs_0_), channel_id=1, source_target_pairs={{0,6},{2,0},{4,2},{6,4},{1,7},{3,1},{5,3},{7,5},{8,14},{10,8},{12,... | collective-permute-start | bytes 589832 | tf_op jit(solution)/shard_map/ppermute | solution.py:48
  30.6 10.2 %collective-permute-start.4 = (bf16[64,1536]{1,0:T(8,128)(2,1)}, bf16[64,1536]{1,0:T(8,128)(2,1)}, u32[]{:S(2)}, u32[]{:S(2)}) collective-permute-start(bf16[64,1536]{1,0:T(8,128)(2,1)} %get-tuple-element.48.refs_0_), channel_id=1, source_target_pairs={{0,4},{2,6},{4,0},{6,2},{1,5},{3,7},{5,1},{7,3},{8,12},{10,14},{12... | collective-permute-start | bytes 589832 | tf_op jit(solution)/shard_map/ppermute | solution.py:48
  31.3 11.5 %collective-permute-start.5 = (bf16[64,1536]{1,0:T(8,128)(2,1)}, bf16[64,1536]{1,0:T(8,128)(2,1)}, u32[]{:S(2)}, u32[]{:S(2)}) collective-permute-start(bf16[64,1536]{1,0:T(8,128)(2,1)} %get-tuple-element.48.refs_0_), channel_id=1, source_target_pairs={{0,2},{2,4},{4,6},{6,0},{1,3},{3,5},{5,7},{7,1},{8,10},{10,12},{12... | collective-permute-start | bytes 589832 | tf_op jit(solution)/shard_map/ppermute | solution.py:48
  33.1 7.2 %copy-start.17 = (bf16[64,1536]{1,0:T(8,128)(2,1)S(1)}, bf16[64,1536]{1,0:T(8,128)(2,1)}, u32[]{:S(2)}) copy-start(bf16[64,1536]{1,0:T(8,128)(2,1)} %get-tuple-element.48.refs_0_) | copy-start | bytes 589828
  33.1 9.7 %copy-start.15 = (bf16[64,3840]{1,0:T(8,128)(2,1)S(1)}, bf16[64,3840]{1,0:T(8,128)(2,1)}, u32[]{:S(2)}) copy-start(bf16[64,3840]{1,0:T(8,128)(2,1)} %get-tuple-element.55.refs_0_) | copy-start | bytes 1474564
  34.4 11.1 %copy-start.1 = (bf16[1536,896]{1,0:T(8,128)(2,1)S(1)}, bf16[1536,896]{1,0:T(8,128)(2,1)}, u32[]{:S(2)}) copy-start(bf16[1536,896]{1,0:T(8,128)(2,1)} %gate.3) | copy-start | bytes 8257540
  34.4 22.9 %all-to-all-start = ((f32[8,48,896]{2,1,0:T(8,128)}), f32[8,48,896]{2,1,0:T(8,128)}, u32[]{:S(2)}, u32[]{:S(2)}) async-start(f32[8,48,896]{2,1,0:T(8,128)} %broadcast_in_dim.2), calls=%async_computation | async-start | bytes 2752512 | tf_op jit(solution)/shard_map/all_to_all | solution.py:56
  40.4 3.4 %collective-permute-start.6 = (bf16[64,1536]{1,0:T(8,128)(2,1)S(1)}, bf16[64,1536]{1,0:T(8,128)(2,1)}, u32[]{:S(2)}, u32[]{:S(2)}) collective-permute-start(bf16[64,1536]{1,0:T(8,128)(2,1)S(1)} %copy-done.17), channel_id=1, source_target_pairs={{0,1},{1,0},{2,3},{3,2},{4,5},{5,4},{6,7},{7,6},{8,9},{9,8},{10,11... | collective-permute-start | bytes 589832 | tf_op jit(solution)/shard_map/ppermute | solution.py:48
  40.4 5.1 %collective-permute-start.7 = (bf16[64,1536]{1,0:T(8,128)(2,1)}, bf16[64,1536]{1,0:T(8,128)(2,1)}, u32[]{:S(2)}, u32[]{:S(2)}) collective-permute-start(bf16[64,1536]{1,0:T(8,128)(2,1)} %collective-permute-done.3.refs_1_), channel_id=1, source_target_pairs={{0,1},{1,0},{2,3},{3,2},{4,5},{5,4},{6,7},{7,6},{8,9},{9,8},{10,11... | collective-permute-start | bytes 589832 | tf_op jit(solution)/shard_map/ppermute | solution.py:48
  40.9 4.6 %collective-permute-start.8 = (bf16[64,1536]{1,0:T(8,128)(2,1)}, bf16[64,1536]{1,0:T(8,128)(2,1)}, u32[]{:S(2)}, u32[]{:S(2)}) collective-permute-start(bf16[64,1536]{1,0:T(8,128)(2,1)} %collective-permute-done.4.refs_2_), channel_id=1, source_target_pairs={{0,1},{1,0},{2,3},{3,2},{4,5},{5,4},{6,7},{7,6},{8,9},{9,8},{10,11... | collective-permute-start | bytes 589832 | tf_op jit(solution)/shard_map/ppermute | solution.py:48
  42.8 2.7 %collective-permute-start.9 = (bf16[64,1536]{1,0:T(8,128)(2,1)}, bf16[64,1536]{1,0:T(8,128)(2,1)}, u32[]{:S(2)}, u32[]{:S(2)}) collective-permute-start(bf16[64,1536]{1,0:T(8,128)(2,1)} %collective-permute-done.5.refs_3_), channel_id=1, source_target_pairs={{0,1},{1,0},{2,3},{3,2},{4,5},{5,4},{6,7},{7,6},{8,9},{9,8},{10,11... | collective-permute-start | bytes 589832 | tf_op jit(solution)/shard_map/ppermute | solution.py:48
  42.9 20.2 %collective-permute-start.10 = (bf16[64,3840]{1,0:T(8,128)(2,1)S(1)}, bf16[64,3840]{1,0:T(8,128)(2,1)}, u32[]{:S(2)}, u32[]{:S(2)}) collective-permute-start(bf16[64,3840]{1,0:T(8,128)(2,1)S(1)} %copy-done.15), channel_id=1, source_target_pairs={{0,6},{2,0},{4,2},{6,4},{1,7},{3,1},{5,3},{7,5},{8,14},{10,8},{12,... | collective-permute-start | bytes 1474568 | tf_op jit(solution)/shard_map/ppermute | solution.py:48
  43.8 19.3 %collective-permute-start.11 = (bf16[64,3840]{1,0:T(8,128)(2,1)S(1)}, bf16[64,3840]{1,0:T(8,128)(2,1)}, u32[]{:S(2)}, u32[]{:S(2)}) collective-permute-start(bf16[64,3840]{1,0:T(8,128)(2,1)S(1)} %copy-done.15), channel_id=1, source_target_pairs={{0,4},{2,6},{4,0},{6,2},{1,5},{3,7},{5,1},{7,3},{8,12},{10,14},{12... | collective-permute-start | bytes 1474568 | tf_op jit(solution)/shard_map/ppermute | solution.py:48
  45.5 23.5 %collective-permute-start.12 = (bf16[64,3840]{1,0:T(8,128)(2,1)S(1)}, bf16[64,3840]{1,0:T(8,128)(2,1)}, u32[]{:S(2)}, u32[]{:S(2)}) collective-permute-start(bf16[64,3840]{1,0:T(8,128)(2,1)S(1)} %copy-done.15), channel_id=1, source_target_pairs={{0,2},{2,4},{4,6},{6,0},{1,3},{3,5},{5,7},{7,1},{8,10},{10,12},{12... | collective-permute-start | bytes 1474568 | tf_op jit(solution)/shard_map/ppermute | solution.py:48
  45.5 1.8 copy-start.3
  54.6 1.2 copy-start.8
  57.3 15.9 %copy-start.9 = (bf16[512,1536]{1,0:T(8,128)(2,1)S(1)}, bf16[512,1536]{1,0:T(8,128)(2,1)}, u32[]{:S(2)}) copy-start(bf16[512,1536]{1,0:T(8,128)(2,1)} %copy-done.8) | copy-start | bytes 4718596
  57.3 28.7 %all-to-all-start.1 = ((f16[8,64,1792]{2,1,0:T(8,128)(2,1)}), f16[8,64,1792]{2,1,0:T(8,128)(2,1)}, u32[]{:S(2)}, u32[]{:S(2)}) async-start(f16[8,64,1792]{2,1,0:T(8,128)(2,1)} %bitcast.10), calls=%async_computation.1 | async-start | bytes 3670016 | tf_op jit(solution)/shard_map/all_to_all | solution.py:56
  69.0 2.4 %collective-permute-start.13 = (bf16[64,3840]{1,0:T(8,128)(2,1)S(1)}, bf16[64,3840]{1,0:T(8,128)(2,1)S(1)}, u32[]{:S(2)}, u32[]{:S(2)}) collective-permute-start(bf16[64,3840]{1,0:T(8,128)(2,1)S(1)} %copy-done.15), channel_id=1, source_target_pairs={{0,1},{1,0},{2,3},{3,2},{4,5},{5,4},{6,7},{7,6},{8,9},{9,8},{10,11... | collective-permute-start | bytes 1474568 | tf_op jit(solution)/shard_map/ppermute | solution.py:48
  69.0 2.8 %collective-permute-start.14 = (bf16[64,3840]{1,0:T(8,128)(2,1)}, bf16[64,3840]{1,0:T(8,128)(2,1)S(1)}, u32[]{:S(2)}, u32[]{:S(2)}) collective-permute-start(bf16[64,3840]{1,0:T(8,128)(2,1)} %collective-permute-done.10.refs_1_), channel_id=1, source_target_pairs={{0,1},{1,0},{2,3},{3,2},{4,5},{5,4},{6,7},{7,6},{8,9},{9,8},{10,11... | collective-permute-start | bytes 1474568 | tf_op jit(solution)/shard_map/ppermute | solution.py:48
  69.5 3.0 %collective-permute-start.15 = (bf16[64,3840]{1,0:T(8,128)(2,1)}, bf16[64,3840]{1,0:T(8,128)(2,1)S(1)}, u32[]{:S(2)}, u32[]{:S(2)}) collective-permute-start(bf16[64,3840]{1,0:T(8,128)(2,1)} %collective-permute-done.11.refs_2_), channel_id=1, source_target_pairs={{0,1},{1,0},{2,3},{3,2},{4,5},{5,4},{6,7},{7,6},{8,9},{9,8},{10,11... | collective-permute-start | bytes 1474568 | tf_op jit(solution)/shard_map/ppermute | solution.py:48
  69.5 3.7 %collective-permute-start.16 = (bf16[64,3840]{1,0:T(8,128)(2,1)}, bf16[64,3840]{1,0:T(8,128)(2,1)S(1)}, u32[]{:S(2)}, u32[]{:S(2)}) collective-permute-start(bf16[64,3840]{1,0:T(8,128)(2,1)} %collective-permute-done.12.refs_3_), channel_id=1, source_target_pairs={{0,1},{1,0},{2,3},{3,2},{4,5},{5,4},{6,7},{7,6},{8,9},{9,8},{10,11... | collective-permute-start | bytes 1474568 | tf_op jit(solution)/shard_map/ppermute | solution.py:48
  73.2 1.8 copy-start.14
  75.0 1.0 copy-start.16
  83.3 1.4 copy-start.5
  86.0 24.0 %all-to-all-start.2 = ((f16[8,64,1408]{2,1,0:T(8,128)(2,1)}), f16[8,64,1408]{2,1,0:T(8,128)(2,1)}, u32[]{:S(2)}, u32[]{:S(2)}) async-start(f16[8,64,1408]{2,1,0:T(8,128)(2,1)} %bitcast.11), calls=%async_computation.2 | async-start | bytes 2883584 | tf_op jit(solution)/shard_map/all_to_all | solution.py:56
  110.0 2.5 %copy-start = (f32[8,64,1792]{2,1,0:T(8,128)S(1)}, f32[8,64,1792]{2,1,0:T(8,128)}, u32[]{:S(2)}) copy-start(f32[8,64,1792]{2,1,0:T(8,128)} %convert_element_type.17.first) | copy-start | bytes 11010052
  114.3 1.2 copy-start.7
  116.4 27.1 %all-to-all-start.3 = ((bf16[8,64,1792]{2,1,0:T(8,128)(2,1)}), bf16[8,64,1792]{2,1,0:T(8,128)(2,1)S(1)}, u32[]{:S(2)}, u32[]{:S(2)}) async-start(bf16[8,64,1792]{2,1,0:T(8,128)(2,1)} %copy-done.7), calls=%async_computation.3 | async-start | bytes 3670016 | tf_op jit(solution)/shard_map/all_to_all | solution.py:56
  122.0 1.3 collective-permute-start.17
  123.3 7.1 %collective-permute-start.20 = (f32[64,384]{1,0:T(8,128)S(1)}, f32[64,384]{1,0:T(8,128)S(1)}, u32[]{:S(2)}, u32[]{:S(2)}) collective-permute-start(f32[64,384]{1,0:T(8,128)S(1)} %add.23), channel_id=1, source_target_pairs={{0,4},{2,6},{4,0},{6,2},{1,5},{3,7},{5,1},{7,3},{8,12},{10,14},{12... | collective-permute-start | bytes 294920 | tf_op jit(solution)/shard_map/ppermute | solution.py:48
  125.3 5.2 %collective-permute-start.18 = (f32[64,384]{1,0:T(8,128)S(1)}, f32[64,384]{1,0:T(8,128)S(1)}, u32[]{:S(2)}, u32[]{:S(2)}) collective-permute-start(f32[64,384]{1,0:T(8,128)S(1)} %add.23), channel_id=1, source_target_pairs={{0,6},{2,0},{4,2},{6,4},{1,7},{3,1},{5,3},{7,5},{8,14},{10,8},{12,... | collective-permute-start | bytes 294920 | tf_op jit(solution)/shard_map/ppermute | solution.py:48
  126.1 6.0 %collective-permute-start.19 = (f32[64,384]{1,0:T(8,128)S(1)}, f32[64,384]{1,0:T(8,128)S(1)}, u32[]{:S(2)}, u32[]{:S(2)}) collective-permute-start(f32[64,384]{1,0:T(8,128)S(1)} %add.23), channel_id=1, source_target_pairs={{0,2},{2,4},{4,6},{6,0},{1,3},{3,5},{5,7},{7,1},{8,10},{10,12},{12... | collective-permute-start | bytes 294920 | tf_op jit(solution)/shard_map/ppermute | solution.py:48
  143.5 24.6 %all-to-all-start.4 = ((bf16[8,112,896]{2,1,0:T(8,128)(2,1)}), bf16[8,112,896]{2,1,0:T(8,128)(2,1)S(1)}, u32[]{:S(2)}, u32[]{:S(2)}) async-start(bf16[8,112,896]{2,1,0:T(8,128)(2,1)} %shard_map.169), calls=%async_computation.4 | async-start | bytes 3211264 | tf_op jit(solution)/shard_map/all_to_all | solution.py:56
  149.1 1.8 copy-start.2
  150.9 1.8 copy-start.4
  154.5 3.5 %collective-permute-start.21 = (f32[256,1536]{1,0:T(8,128)S(1)}, f32[256,1536]{1,0:T(8,128)S(1)}, u32[]{:S(2)}, u32[]{:S(2)}) collective-permute-start(f32[256,1536]{1,0:T(8,128)S(1)} %shard_map.171), channel_id=1, source_target_pairs={{0,1},{1,0},{2,3},{3,2},{4,5},{5,4},{6,7},{7,6},{8,9},{9,8},{10,11... | collective-permute-start | bytes 4718600 | tf_op jit(solution)/shard_map/ppermute | solution.py:48
  156.4 11.6 %copy-start.11 = (bf16[384,512]{1,0:T(8,128)(2,1)S(1)}, bf16[384,512]{1,0:T(8,128)(2,1)}, u32[]{:S(2)}) copy-start(bf16[384,512]{1,0:T(8,128)(2,1)} %copy-done.10) | copy-start | bytes 1179652
  159.0 12.6 %collective-permute-start.22 = (bf16[64,1536]{1,0:T(8,128)(2,1)}, bf16[64,1536]{1,0:T(8,128)(2,1)S(1)}, u32[]{:S(2)}, u32[]{:S(2)}) collective-permute-start(bf16[64,1536]{1,0:T(8,128)(2,1)} %get-tuple-element.79), channel_id=1, source_target_pairs={{0,2},{2,4},{4,6},{6,0},{1,3},{3,5},{5,7},{7,1},{8,10},{10,12},{12... | collective-permute-start | bytes 589832 | tf_op jit(solution)/shard_map/ppermute | solution.py:52
  159.0 12.6 %collective-permute-start.23 = (bf16[64,1536]{1,0:T(8,128)(2,1)S(1)}, bf16[64,1536]{1,0:T(8,128)(2,1)S(1)}, u32[]{:S(2)}, u32[]{:S(2)}) collective-permute-start(bf16[64,1536]{1,0:T(8,128)(2,1)S(1)} %get-tuple-element.80), channel_id=1, source_target_pairs={{0,6},{2,0},{4,2},{6,4},{1,7},{3,1},{5,3},{7,5},{8,14},{10,8},{12,... | collective-permute-start | bytes 589832 | tf_op jit(solution)/shard_map/ppermute | solution.py:52
  162.2 9.3 %collective-permute-start.24 = (bf16[64,1536]{1,0:T(8,128)(2,1)S(1)}, bf16[64,1536]{1,0:T(8,128)(2,1)S(1)}, u32[]{:S(2)}, u32[]{:S(2)}) collective-permute-start(bf16[64,1536]{1,0:T(8,128)(2,1)S(1)} %get-tuple-element.81), channel_id=1, source_target_pairs={{0,4},{2,6},{4,0},{6,2},{1,5},{3,7},{5,1},{7,3},{8,12},{10,14},{12... | collective-permute-start | bytes 589832 | tf_op jit(solution)/shard_map/ppermute | solution.py:52
  168.1 1.7 copy-start.6
  172.4 19.7 %copy-start.13 = (f32[16,2688]{1,0:T(8,128)}, f32[16,2688]{1,0:T(8,128)S(1)}, u32[]{:S(2)}) copy-start(f32[16,2688]{1,0:T(8,128)S(1)} %get-tuple-element.83.kept) | copy-start | bytes 516100
  172.4 19.7 %all-to-all-start.5 = ((bf16[4,16,2688]{2,1,0:T(8,128)(2,1)}), bf16[4,16,2688]{2,1,0:T(8,128)(2,1)S(1)}, u32[]{:S(2)}, u32[]{:S(2)}) async-start(bf16[4,16,2688]{2,1,0:T(8,128)(2,1)} %get-tuple-element.84), calls=%async_computation.5 | async-start | bytes 688128 | tf_op jit(solution)/shard_map/all_to_all | solution.py:56
  (5 other events, 3.7 us)
